TPU v7x, 256 devices: a whole 4x4x8 slice. The times are simulated.
256 devices in a mesh: seq: 16 (over z, x_lo), wt: 16 (over x_hi, y, core).
Axes of the slice: x: 4 (x_hi: 2, x_lo: 2; x = x_hi * 2 + x_lo), y: 4, z: 8, core: 2. Of those that a mesh axis runs over, the one named last changes fastest.
Arguments:
- frames: bfloat16 [4096, 4096], P('seq'), may hold values from -40 to 40
- attn_norm_gain: float32 [4096], replicated, may hold values from 0.1 to 1.9
- qkv_weight: bfloat16 [3, 4096, 4096], P(None, 'seq', 'wt'), may hold values from -4 to 4
- attn_out_weight: bfloat16 [4096, 4096], P('seq', 'wt'), may hold values from -0.125 to 0.125
- conv_norm_gain: float32 [4096], replicated, may hold values from 0.1 to 1.9
- glu_weight: bfloat16 [2, 4096, 4096], P(None, 'seq', 'wt'), may hold values from -0.09375 to 0.09375
- depth_kernel: float32 [31, 4096], P(None, 'wt'), may hold values from -1 to 1
- norm_scale: float32 [4096], P('wt'), may hold values from 0.5 to 2
- norm_shift: float32 [4096], P('wt'), may hold values from -3 to 3
- conv_out_weight: bfloat16 [4096, 4096], P('seq', 'wt'), may hold values from -0.125 to 0.125
Outputs:
- encoded: bfloat16 [4096, 4096], P('seq', 'wt')
All inputs are finite; a program needn't handle non-finite values.
Results may differ from a plain program's by a relative error of at most 0.014.
Values may be sent and summed in bfloat16 or wider, within the bound.
No kernel may reach another device: no remote copies, remote signals or barrier semaphores. Data moves between devices by JAX's collectives and lax.ppermute only.
A program may use at most 64 MiB of HBM per device.

v0:
```python
import jax
import jax.numpy as jnp
from jax import lax
from jax.sharding import PartitionSpec as P

HEAD_DIM = 128


def padded_2(value, sides, width):
    for axis, dim in sides:
        devices, length = (lax.axis_size(axis), value.shape[dim])
        up = [(i, (i + 1) % devices) for i in range(devices - 1)]
        down = [(j, i) for i, j in up]
        last = lax.slice_in_dim(value, length - width, length, axis=dim)
        first = lax.slice_in_dim(value, 0, width, axis=dim)
        before = lax.ppermute(last, axis, up)
        after = lax.ppermute(first, axis, down)
        value = jnp.concatenate([before, value, after], axis=dim)
    return value


def norm_rows(values, gain_vec):
    wide = values.astype(jnp.float32)
    row_mean = jnp.mean(wide, axis=-1, keepdims=True)
    centered = wide - row_mean
    row_var = jnp.mean(centered * centered, axis=-1, keepdims=True)
    return (centered * lax.rsqrt(row_var + 1e-05) * gain_vec).astype(jnp.bfloat16)


def project_in(normed, stacked):
    return jnp.einsum(
        "rd,mdc->rmc",
        normed,
        lax.all_gather(stacked, "seq", axis=1, tiled=True),
        preferred_element_type=jnp.float32,
    )


def project_out(inputs, weight):
    return lax.dot_general(
        inputs,
        lax.all_gather(weight, "seq", axis=0, tiled=True),
        (((1,), (1,)), ((), ())),
        preferred_element_type=jnp.float32,
    )


def feature_share(partial_sums):
    return lax.psum_scatter(
        partial_sums.astype(jnp.bfloat16), "wt", scatter_dimension=1, tiled=True
    ).astype(jnp.float32)


def local(
    frames,
    attn_norm_gain,
    qkv_weight,
    attn_out_weight,
    conv_norm_gain,
    glu_weight,
    depth_kernel,
    norm_scale,
    norm_shift,
    conv_out_weight,
):
    row_count = frames.shape[0]
    col_count = qkv_weight.shape[2]
    heads_here = col_count // HEAD_DIM
    column_start = lax.axis_index("wt") * col_count
    normed = norm_rows(frames, attn_norm_gain)
    projected = project_in(normed, qkv_weight).astype(jnp.bfloat16)
    query_heads = projected[:, 0].reshape(row_count, heads_here, HEAD_DIM)
    keys = projected[:, 1]
    values = projected[:, 2]
    score_scale = HEAD_DIM ** (-0.5)
    key_segment = lax.all_gather(keys, "seq", axis=0, tiled=True)
    value_segment = lax.all_gather(values, "seq", axis=0, tiled=True)
    row_best = jnp.full((heads_here, row_count), -1e30, jnp.float32)
    key_heads = key_segment.reshape(key_segment.shape[0], heads_here, HEAD_DIM)
    value_heads = value_segment.reshape(value_segment.shape[0], heads_here, HEAD_DIM)
    scores = (
        jnp.einsum("qhd,khd->hqk", query_heads, key_heads, preferred_element_type=jnp.float32)
        * score_scale
    )
    new_best = jnp.maximum(row_best, jnp.max(scores, axis=-1))
    exp_weights = jnp.exp(scores - new_best[..., None])
    running_sum = jnp.sum(exp_weights, axis=-1)
    weighted = jnp.einsum(
        "hqk,khd->hqd",
        exp_weights.astype(jnp.bfloat16),
        value_heads,
        preferred_element_type=jnp.float32,
    )
    row_best, running_sum, weighted = (new_best, running_sum, weighted)
    context = (
        (weighted / running_sum[..., None])
        .transpose(1, 0, 2)
        .reshape(row_count, col_count)
        .astype(jnp.bfloat16)
    )
    attended = project_out(context, attn_out_weight)
    share_cols = feature_share(attended)
    frame_cols = lax.dynamic_slice_in_dim(frames, column_start, col_count, 1)
    residual_cols = (frame_cols.astype(jnp.float32) + share_cols).astype(jnp.bfloat16)
    residual_full = lax.all_gather(residual_cols, "wt", axis=1, tiled=True)
    normed_conv = norm_rows(residual_full, conv_norm_gain)
    glu_pair = project_in(normed_conv, glu_weight)
    gated = (glu_pair[:, 0] * jax.nn.sigmoid(glu_pair[:, 1])).astype(jnp.bfloat16)
    rim_width = (depth_kernel.shape[0] - 1) // 2
    padded = padded_2(gated, (("seq", 0),), rim_width).astype(jnp.float32)
    depth_out = jnp.zeros((row_count, col_count), jnp.float32)
    for tap_index in range(depth_kernel.shape[0]):
        depth_out = depth_out + depth_kernel[tap_index] * padded[tap_index : tap_index + row_count]
    shifted = depth_out * norm_scale + norm_shift
    activated = (shifted * jax.nn.sigmoid(shifted)).astype(jnp.bfloat16)
    conv_cols = feature_share(project_out(activated, conv_out_weight))
    residual_cols = lax.dynamic_slice_in_dim(residual_full, column_start, col_count, 1)
    return (residual_cols.astype(jnp.float32) + conv_cols).astype(jnp.bfloat16)


def solution(mesh):
    in_specs = (
        P("seq", None),
        P(),
        P(None, "seq", "wt"),
        P("seq", "wt"),
        P(),
        P(None, "seq", "wt"),
        P(None, "wt"),
        P("wt"),
        P("wt"),
        P("seq", "wt"),
    )
    out_specs = P("seq", "wt")
    return jax.shard_map(local, mesh=mesh, in_specs=in_specs, out_specs=out_specs, check_vma=False)
```

profile of v0, /device:TPU:1, one launch (start us, length us, event | category | flops | bytes accessed | tf_op | source)
XLA Modules:
  0.0 818.7 jit_solution(16398674720940230616)
XLA Ops:
  6.5 2.1 copy.11
  8.7 2.0 convert_reduce_fusion.1
  11.4 154.0 %all-gather.10.cloned.1.call-done = bf16[3,4096,256]{1,2,0:T(8,128)(2,1)} async-done(((bf16[3,256,256]{1,2,0:T(8,128)(2,1)}), bf16[3,4096,256]{1,2,0:T(8,128)(2,1)}) %all-gather.10.cloned.1.call-update) | async-done | bytes 6291472 | tf_op jit(solution)/shard_map/all_gather | solution.py:34
  165.4 4.7 fusion.28
  172.2 79.4 %all-gather.20.cloned.1.call-done = bf16[4096,1,256]{0,2,1:T(8,128)(2,1)} async-done(((bf16[256,1,256]{0,2,1:T(8,128)(2,1)}), bf16[4096,1,256]{0,2,1:T(8,128)(2,1)}) %all-gather.20.cloned.1.call-update) | async-done | bytes 2097168 | tf_op jit(solution)/shard_map/all_gather | solution.py:76
  251.6 3.0 multiply_reduce_fusion
  254.6 3.2 copy-done
  259.3 77.6 %all-gather.22.cloned.1.call-done = bf16[4096,1,256]{0,2,1:T(8,128)(2,1)} async-done(((bf16[256,1,256]{0,2,1:T(8,128)(2,1)}), bf16[4096,1,256]{0,2,1:T(8,128)(2,1)}) %all-gather.22.cloned.1.call-update) | async-done | bytes 2097168 | tf_op jit(solution)/shard_map/all_gather | solution.py:77
  337.0 5.8 fusion.37
  342.8 70.1 %all-gather.12.cloned.1.call-done = bf16[4096,256]{1,0:T(8,128)(2,1)} async-done(((bf16[256,256]{1,0:T(8,128)(2,1)}), bf16[4096,256]{1,0:T(8,128)(2,1)}) %all-gather.12.cloned.1.call-update) | async-done | bytes 2097168 | tf_op jit(solution)/shard_map/all_gather | solution.py:42
  412.9 3.7 convolution_convert_fusion.1
  416.6 84.2 %reduce-scatter.3.cloned.1.call-done = bf16[256,256]{1,0:T(8,128)(2,1)} async-done(((bf16[256,4096]{1,0:T(8,128)(2,1)}), bf16[256,256]{1,0:T(8,128)(2,1)}) %reduce-scatter.3.cloned.1.call-update) | async-done | bytes 131088 | tf_op jit(solution)/shard_map/reduce_scatter | solution.py:49
  500.8 1.6 add_convert_fusion.1
  504.1 53.0 %all-gather.14.cloned.1.call-done = bf16[256,4096]{1,0:T(8,128)(2,1)} async-done(((bf16[256,256]{1,0:T(8,128)(2,1)}), bf16[256,4096]{1,0:T(8,128)(2,1)}) %all-gather.14.cloned.1.call-update) | async-done | bytes 2097168 | tf_op jit(solution)/shard_map/all_gather | solution.py:105
  557.1 2.1 convert_reduce_fusion
  559.2 2.3 fusion.6
  561.5 92.5 %all-gather.16.cloned.1.call-done = bf16[2,4096,256]{2,1,0:T(8,128)(2,1)} async-done(((bf16[2,256,256]{2,1,0:T(8,128)(2,1)}), bf16[2,4096,256]{2,1,0:T(8,128)(2,1)}) %all-gather.16.cloned.1.call-update) | async-done | bytes 4194320 | tf_op jit(solution)/shard_map/all_gather | solution.py:34
  654.0 3.5 fusion.20
  657.6 3.6 collective-permute-start
  662.6 3.0 collective-permute-done.1
  665.7 56.0 %all-gather.18.cloned.1.call-done = bf16[4096,256]{1,0:T(8,128)(2,1)} async-done(((bf16[256,256]{1,0:T(8,128)(2,1)}), bf16[4096,256]{1,0:T(8,128)(2,1)}) %all-gather.18.cloned.1.call-update) | async-done | bytes 2097168 | tf_op jit(solution)/shard_map/all_gather | solution.py:42
  721.6 4.6 convolution_convert_fusion
  726.2 84.4 %reduce-scatter.5.cloned.1.call-done = bf16[256,256]{1,0:T(8,128)(2,1)} async-done(((bf16[256,4096]{1,0:T(8,128)(2,1)}), bf16[256,256]{1,0:T(8,128)(2,1)}) %reduce-scatter.5.cloned.1.call-update) | async-done | bytes 131088 | tf_op jit(solution)/shard_map/reduce_scatter | solution.py:49
  810.6 1.6 add_convert_fusion
  (49 shorter events, 7.5 us)
Async XLA Ops:
  6.5 4.1 copy-start.1
  6.5 158.8 %copy-start.4 = (f32[4096]{0:T(1024)S(1)}, f32[4096]{0:T(1024)}, u32[]{:S(2)}) copy-start(f32[4096]{0:T(1024)} %param.11) | copy-start | bytes 49156
  6.5 158.8 %all-gather.10.cloned.1.call-start = ((), (), s32[]{:S(2)}) async-start(), calls=%async_computation.2 | async-start | bytes 6684672 | tf_op jit(solution)/shard_map/all_gather | solution.py:34
  8.6 242.9 %all-gather.20.cloned.1.call-start = ((), (), s32[]{:S(2)}) async-start(), calls=%async_computation.9 | async-start | bytes 2228224 | tf_op jit(solution)/shard_map/all_gather | solution.py:76
  170.8 166.1 %all-gather.22.cloned.1.call-start = ((), (), s32[]{:S(2)}) async-start(), calls=%async_computation.10 | async-start | bytes 2228224 | tf_op jit(solution)/shard_map/all_gather | solution.py:77
  171.6 241.3 %all-gather.12.cloned.1.call-start = ((), (), s32[]{:S(2)}) async-start(), calls=%async_computation.3 | async-start | bytes 2228224 | tf_op jit(solution)/shard_map/all_gather | solution.py:42
  172.1 328.7 %reduce-scatter.3.cloned.1.call-start = ((), (), s32[]{:S(2)}) async-start(), calls=%async_computation.4 | async-start | bytes 2228224 | tf_op jit(solution)/shard_map/reduce_scatter | solution.py:49
  254.6 3.2 copy-start
  342.8 161.2 %copy-start.3 = (f32[31,256]{1,0:T(8,128)S(1)}, f32[31,256]{1,0:T(8,128)}, u32[]{:S(2)}) copy-start(f32[31,256]{1,0:T(8,128)} %param.16) | copy-start | bytes 95236
  416.6 237.4 %copy-start.5 = (f32[4096]{0:T(1024)S(1)}, f32[4096]{0:T(1024)}, u32[]{:S(2)}) copy-start(f32[4096]{0:T(1024)} %param.14) | copy-start | bytes 49156
  416.6 140.5 %all-gather.14.cloned.1.call-start = ((), (), s32[]{:S(2)}) async-start(), calls=%async_computation.5 | async-start | bytes 2228224 | tf_op jit(solution)/shard_map/all_gather | solution.py:105
  502.4 151.6 %all-gather.16.cloned.1.call-start = ((), (), s32[]{:S(2)}) async-start(), calls=%async_computation.6 | async-start | bytes 4456448 | tf_op jit(solution)/shard_map/all_gather | solution.py:34
  503.2 218.4 %all-gather.18.cloned.1.call-start = ((), (), s32[]{:S(2)}) async-start(), calls=%async_computation.7 | async-start | bytes 2228224 | tf_op jit(solution)/shard_map/all_gather | solution.py:42
  503.9 306.7 %reduce-scatter.5.cloned.1.call-start = ((), (), s32[]{:S(2)}) async-start(), calls=%async_computation.8 | async-start | bytes 2228224 | tf_op jit(solution)/shard_map/reduce_scatter | solution.py:49
  557.1 96.9 %copy-start.2 = (bf16[256,4096]{1,0:T(8,128)(2,1)S(1)}, bf16[256,4096]{1,0:T(8,128)(2,1)}, u32[]{:S(2)}) copy-start(bf16[256,4096]{1,0:T(8,128)(2,1)} %all-gather.14.cloned.1.call-done) | copy-start | bytes 6291460
  561.5 160.2 %copy-start.6 = (f32[256]{0:T(256)S(1)}, f32[256]{0:T(256)}, u32[]{:S(2)}) copy-start(f32[256]{0:T(256)} %param.18) | copy-start | bytes 3076
  561.5 160.1 %copy-start.7 = (f32[256]{0:T(256)S(1)}, f32[256]{0:T(256)}, u32[]{:S(2)}) copy-start(f32[256]{0:T(256)} %param.17) | copy-start | bytes 3076
  657.6 5.0 collective-permute-start
  661.2 4.4 collective-permute-start.1
Sparse Core Ops, SparseCore 0:
  9.1 156.2 all-gather.9
  170.9 80.5 all-gather.19
  253.3 83.6 all-gather.21
  338.6 74.2 all-gather.11
  416.9 83.8 reduce-scatter.2
  503.6 53.4 all-gather.13
  559.0 94.9 all-gather.15
  655.9 65.6 all-gather.17
  726.4 84.1 reduce-scatter.4
where the time goes:
time: 820 us; the launch traced here: 819 us
  waiting for transfers between devices  757 us (92%)
  matrix products  25.2 us (3%)
  between operations  13.4 us (2%)
  other arithmetic  11.9 us (1%)
    all_gather x2, waiting for transfers between devices, project_in(): lax.all_gather(stacked, 'seq', axis=1, tiled=True)  246 us
    reduce_scatter x2, waiting for transfers between devices, feature_share(): lax.psum_scatter(partial_sums.astype(jnp.bfloat16), 'wt', scatter_dimensi...  169 us
    all_gather x2, waiting for transfers between devices, project_out(): lax.all_gather(weight, 'seq', axis=0, tiled=True)  126 us
    all_gather x1, waiting for transfers between devices, local(): key_segment = lax.all_gather(keys, 'seq', axis=0, tiled=True)  79.4 us
    all_gather x1, waiting for transfers between devices, local(): value_segment = lax.all_gather(values, 'seq', axis=0, tiled=True)  77.6 us
    all_gather x1, waiting for transfers between devices, local(): residual_full = lax.all_gather(residual_cols, 'wt', axis=1, tiled=True)  53 us
  transfers between devices with their start and end apart: 11, of which 10 were waited for; matrix products, arithmetic and copies ran while one was open for 3% of the time, Pallas kernels for 0%

commit v1 on v0

v1 whole, which is shorter than its diff:
```python
import jax
import jax.numpy as jnp
from jax import lax
from jax.experimental import pallas as pl
from jax.experimental.pallas import tpu as pltpu
from jax.sharding import Mesh, PartitionSpec as P

HEAD_DIM = 128
BF16 = jnp.bfloat16
F32 = jnp.float32
SEQ = ("z", "xl")
WT = ("xh", "y", "c")
CHIPS = ("xh", "y")


def shift(value, axis, step):
    count = lax.axis_size(axis)
    return lax.ppermute(value, axis, [(i, (i + step) % count) for i in range(count)])


def smem():
    return pl.BlockSpec(memory_space=pltpu.SMEM)


def vmem():
    return pl.BlockSpec(memory_space=pltpu.VMEM)


def run_kernel(body, where, arrays, outs, scratch, megabytes, flops, moved, exps=0):
    return pl.pallas_call(
        body,
        out_shape=outs,
        in_specs=[smem()] + [vmem()] * len(arrays),
        out_specs=jax.tree.map(lambda _: vmem(), outs),
        scratch_shapes=scratch,
        compiler_params=pltpu.CompilerParams(vmem_limit_bytes=megabytes << 20),
        cost_estimate=pl.CostEstimate(flops=flops, bytes_accessed=moved, transcendentals=exps),
    )(where, *arrays)


def dot(a, b):
    return jnp.dot(a, b, preferred_element_type=F32)


def dot_t(a, b):
    return lax.dot_general(a, b, (((1,), (1,)), ((), ())), preferred_element_type=F32)


def norm_blocks_kernel(where, frames, gain, mine, other):
    rows, width = frames.shape
    blocks = mine.shape[0]
    block = mine.shape[2]
    z, xl = where[0], where[1]
    step_rows = 32

    def chunk(i, carry):
        r = pl.ds(pl.multiple_of(i * step_rows, step_rows), step_rows)
        wide = frames[r, :].astype(F32)
        mean = jnp.mean(wide, axis=-1, keepdims=True)
        centered = wide - mean
        scale = lax.rsqrt(jnp.mean(centered * centered, axis=-1, keepdims=True) + 1e-05)
        for j in range(blocks):
            owner = lax.rem(z + j, blocks) * 2
            for out, parity in ((mine, xl), (other, 1 - xl)):
                cols = pl.ds(pl.multiple_of((owner + parity) * block, block), block)
                part = (frames[r, cols].astype(F32) - mean) * scale * gain[:, cols]
                out[j, r, :] = part.astype(BF16)
        return carry

    lax.fori_loop(0, rows // step_rows, chunk, 0)


def project_kernel(where, mine, got, *refs):
    pieces, (keep, send) = refs[:-2], refs[-2:]
    xl = where[1]
    for m in range(3):
        for r, a in enumerate((mine, got)):
            acc = None
            for j in range(8):
                if j < 4:
                    term = dot(a[j], pieces[j][m])
                elif j == 4:
                    half = pieces[4].shape[1]
                    term = dot(a[4][:, :half], pieces[4][m]) + dot(a[4][:, half:], pieces[5][m])
                else:
                    term = dot(a[j], pieces[j + 1][m])
                acc = term if acc is None else acc + term
            low, high = acc[:, :HEAD_DIM], acc[:, HEAD_DIM:]
            keep[m, r] = jnp.where(xl == 0, low, high)
            send[m, r] = jnp.where(xl == 0, high, low).astype(BF16)


def attend_kernel(where, q_keep, q_got, *refs):
    parts, (mine, send), scores = refs[:-3], refs[-3:-1], refs[-1]
    scale = HEAD_DIM ** (-0.5)
    keys, values = parts[0::2], parts[1::2]
    step_rows = 128
    chunk = keys[0].shape[1] * 2
    for r, out in enumerate((mine, send)):
        for i in range(0, q_keep.shape[2], step_rows):
            query = (q_keep[0, r, i : i + step_rows] + q_got[0, 1 - r, i : i + step_rows].astype(F32)).astype(BF16)
            best = None
            for j, key in enumerate(keys):
                part = dot_t(query, key[...].reshape(chunk, HEAD_DIM))
                scores[:, j * chunk : (j + 1) * chunk] = part
                top = jnp.max(part, axis=-1, keepdims=True)
                best = top if best is None else jnp.maximum(best, top)
            total = jnp.zeros((step_rows, 1), F32)
            acc = jnp.zeros((step_rows, HEAD_DIM), F32)
            for j, value in enumerate(values):
                weights = jnp.exp((scores[:, j * chunk : (j + 1) * chunk] - best) * scale)
                total = total + jnp.sum(weights, axis=-1, keepdims=True)
                acc = acc + dot(weights.astype(BF16), value[...].reshape(chunk, HEAD_DIM))
            out[i : i + step_rows, :] = (acc / total).astype(BF16)


def spread_out(inputs, weight, mine, other, core):
    blocks, rows, block = mine.shape
    for j in range(blocks):
        for out, parity in ((mine, core), (other, 1 - core)):
            at = pl.ds(pl.multiple_of((2 * j + parity) * block, block), block)
            out[j] = dot_t(inputs, weight[at, :]).astype(BF16)


def project_out_kernel(where, own, got, weight, mine, other):
    xl = where[1]
    a, b = own[...], got[...]
    heads = jnp.concatenate([jnp.where(xl == 0, a, b), jnp.where(xl == 0, b, a)], axis=1)
    spread_out(heads, weight, mine, other, where[2])


def glu_kernel(where, mine, other, gain, weight, gated, normed):
    blocks, rows, block = mine.shape
    core = where[2]
    step_rows = 32
    width = 2 * blocks * block

    def chunk(i, carry):
        r = pl.ds(pl.multiple_of(i * step_rows, step_rows), step_rows)
        parts = [ref[j, r, :].astype(F32) for j in range(blocks) for ref in (mine, other)]
        mean = jnp.sum(sum(parts), axis=-1, keepdims=True) / width
        square = sum((p - mean) * (p - mean) for p in parts)
        scale = lax.rsqrt(jnp.sum(square, axis=-1, keepdims=True) / width + 1e-05)
        for n, p in enumerate(parts):
            parity = core if n % 2 == 0 else 1 - core
            cols = pl.ds(pl.multiple_of((n // 2 * 2 + parity) * block, block), block)
            normed[n, r, :] = ((p - mean) * scale * gain[:, cols]).astype(BF16)
        return carry

    lax.fori_loop(0, rows // step_rows, chunk, 0)
    sums = [None, None]
    for n in range(2 * blocks):
        parity = core if n % 2 == 0 else 1 - core
        at = pl.ds(pl.multiple_of((n // 2 * 2 + parity) * block, block), block)
        for m in range(2):
            term = dot(normed[n], weight[m, at, :])
            sums[m] = term if sums[m] is None else sums[m] + term
    gated[...] = (sums[0] * jax.nn.sigmoid(sums[1])).astype(BF16)


def conv_kernel(where, gated, before, after, taps, scale, offset, weight, mine, other, padded, activated):
    rows = gated.shape[0]
    rim = before.shape[0]
    seq = where[0] * 2 + where[1]
    padded[:rim] = jnp.where(seq > 0, before[...].astype(F32), 0.0)
    padded[rim : rim + rows] = gated[...].astype(F32)
    padded[rim + rows :] = jnp.where(seq < where[3] - 1, after[...].astype(F32), 0.0)
    count = taps.shape[0]
    first = rim - (count - 1) // 2
    for i in range(0, rows, 32):
        acc = None
        for k in range(count):
            term = taps[k : k + 1, :] * padded[i + first + k : i + first + k + 32, :]
            acc = term if acc is None else acc + term
        v = acc * scale[...] + offset[...]
        activated[i : i + 32, :] = (v * jax.nn.sigmoid(v)).astype(BF16)
    spread_out(activated[...], weight, mine, other, where[2])


def ring(value, first_half, second_half):
    right = left = value
    ahead, behind = [], []
    for _ in range(3):
        right = shift(right, "z", 1)
        left = shift(left, "z", -1)
        ahead.append(left)
        behind.append(right)
    far = [shift(first_half(right), "z", 1), shift(second_half(left), "z", -1)]
    return [value] + ahead + far + behind[::-1]


def reduce_features(mine, other):
    got = shift(other, "c", 1)
    pair = (mine.astype(F32) + got.astype(F32)).astype(BF16)
    parts = lax.all_to_all(pair, CHIPS, 0, 0, tiled=True)
    return jnp.sum(parts.astype(F32), axis=0)


def gather_features(value):
    parts = lax.all_to_all(jnp.broadcast_to(value, (8,) + value.shape), CHIPS, 0, 0, tiled=True)
    return parts, shift(parts, "c", 1)


def local(
    frames,
    attn_norm_gain,
    qkv_weight,
    attn_out_weight,
    conv_norm_gain,
    glu_weight,
    depth_kernel,
    norm_scale,
    norm_shift,
    conv_out_weight,
):
    rows, width = frames.shape
    block = qkv_weight.shape[2]
    blocks = width // block // 2
    z, xl, core = (lax.axis_index(a) for a in ("z", "xl", "c"))
    where = jnp.stack([z, xl, core, lax.axis_size(SEQ)]).astype(jnp.int32)
    S = jax.ShapeDtypeStruct

    out_weight = lax.all_gather(attn_out_weight, SEQ, axis=0, tiled=True)
    glu_full = lax.all_gather(glu_weight, SEQ, axis=1, tiled=True)
    conv_weight = lax.all_gather(conv_out_weight, SEQ, axis=0, tiled=True)

    half = block // 2
    pieces = ring(qkv_weight, lambda v: v[:, :half], lambda v: v[:, half:])
    mine, other = run_kernel(
        norm_blocks_kernel, where, [frames, attn_norm_gain.reshape(1, width)],
        [S((blocks, rows, block), BF16)] * 2, [], 16, 10 * rows * width, 4 * rows * width)
    got = shift(other, "xl", 1)
    keep, send = run_kernel(
        project_kernel, where, [mine, got] + pieces,
        [S((3, 2, rows, HEAD_DIM), F32), S((3, 2, rows, HEAD_DIM), BF16)], [], 24,
        6 * rows * width * block, 6 * block * block * 8 + 4 * rows * width)
    kv_got = shift(send[1:], "xl", 1)
    q_got = shift(send[:1], "xl", 1)
    kv = (keep[1:] + kv_got[:, ::-1].astype(F32)).astype(BF16)
    kv_parts = ring(kv, lambda v: v[:1], lambda v: v[1:])
    flat = []
    for j, part in enumerate(kv_parts):
        if j in (4, 5):
            flat.append(part[0])
        else:
            flat += [part[0], part[1]]
    own, away = run_kernel(
        attend_kernel, where, [keep[:1], q_got] + flat,
        [S((rows, HEAD_DIM), BF16)] * 2, [pltpu.VMEM((128, 16 * rows), F32)], 32,
        8 * rows * 16 * rows * HEAD_DIM, 4 << 20, 2 * rows * 16 * rows)
    back = shift(away, "xl", 1)
    blocks_out = [S((blocks, rows, block), BF16)] * 2
    mine, other = run_kernel(
        project_out_kernel, where, [own, back, out_weight], blocks_out, [], 16,
        2 * rows * block * width, 4 << 20)
    frame_cols = lax.dynamic_slice_in_dim(frames, lax.axis_index(WT) * block, block, 1)
    mixed = (frame_cols.astype(F32) + reduce_features(mine, other)).astype(BF16)
    mine, other = gather_features(mixed)
    gated = run_kernel(
        glu_kernel, where, [mine, other, conv_norm_gain.reshape(1, width), glu_full],
        S((rows, block), BF16), [pltpu.VMEM((2 * blocks, rows, block), BF16)], 24,
        4 * rows * block * width, 6 << 20)
    rim = 16
    before = shift(gated[rows - rim :], SEQ, 1)
    after = shift(gated[:rim], SEQ, -1)
    mine, other = run_kernel(
        conv_kernel, where,
        [gated, before, after, depth_kernel, norm_scale.reshape(1, block), norm_shift.reshape(1, block), conv_weight],
        blocks_out, [pltpu.VMEM((rows + 2 * rim, block), F32), pltpu.VMEM((rows, block), BF16)], 16,
        2 * rows * block * width, 4 << 20)
    return (mixed.astype(F32) + reduce_features(mine, other)).astype(BF16)


def solution(mesh):
    split = Mesh(mesh.devices.reshape(8, 2, 2, 4, 2), ("z", "xl", "xh", "y", "c"))
    in_specs = (
        P(SEQ, None),
        P(),
        P(None, SEQ, WT),
        P(SEQ, WT),
        P(),
        P(None, SEQ, WT),
        P(None, WT),
        P(WT),
        P(WT),
        P(SEQ, WT),
    )
    return jax.shard_map(local, mesh=split, in_specs=in_specs, out_specs=P(SEQ, WT), check_vma=False)
```

time: 820 us -> 315 us (0.38)
  waiting for transfers between devices: 757 us -> 164 us
  starting transfers between devices: 5.25 us -> 69.1 us
  blocking collectives: 0 us -> 38.8 us
  matrix products: 25.2 us -> 0 us
  Pallas kernels: 0 us -> 18 us
  other arithmetic: 11.9 us -> 3.6 us
    all_gather x7 -> x3, waiting for transfers between devices: 583 us -> 29.2 us  [the longest x1 29.2 us: local(): conv_weight = lax.all_gather(conv_out_weight, SEQ, axis=0, tiled=True)]
    reduce_scatter x2 -> x0, waiting for transfers between devices: 169 us -> none  [feature_share(): lax.psum_scatter(partial_sums.astype(jnp.bfloat16), 'wt', scatter_dimensi...]
    ppermute x2 -> x25, waiting for transfers between devices: 3 us -> 94.3 us  [shift(): lax.ppermute(value, axis, [(i, (i + step) % count) for i in range(count)])]
    ppermute x2 -> x25, starting transfers between devices: 4.93 us -> 59.6 us  [shift(): lax.ppermute(value, axis, [(i, (i + step) % count) for i in range(count)])]
    all_to_all x0 -> x1, waiting for transfers between devices: none -> 39 us  [reduce_features(): parts = lax.all_to_all(pair, CHIPS, 0, 0, tiled=True)]
    all_to_all x0 -> x2, blocking collectives: none -> 38.8 us  [the longest x1 21.2 us: reduce_features(): parts = lax.all_to_all(pair, CHIPS, 0, 0, tiled=True)]
    dot_general x6 -> x0, matrix products: 25.2 us -> none  [the longest x2 8.25 us: project_out(): lax.dot_general(inputs, lax.all_gather(weight, 'seq', axis=0, tiled=True)...]
    pallas_call x0 -> x6, Pallas kernels: none -> 18 us  [run_kernel(): pl.pallas_call(body, out_shape=outs, in_specs=[smem()] + [vmem()] * len(a...]
  transfers between devices with their start and end apart: 11 -> 29, of which waited for: 10 -> 20; matrix products, arithmetic and copies ran while one was open for 3% -> 1% of each run, Pallas kernels for 0% -> 5%
where the time goes in v1:
time: 315 us
  waiting for transfers between devices  164 us (52%)
  starting transfers between devices  69.1 us (22%)
  blocking collectives  38.8 us (12%)
  Pallas kernels  18 us (6%)
  between operations  13.3 us (4%)
  local copies, waits for them, and re-layouts  8.04 us (3%)
  other arithmetic  3.6 us (1%)
    ppermute x25, waiting for transfers between devices, shift(): lax.ppermute(value, axis, [(i, (i + step) % count) for i in range(count)])  94.3 us
    ppermute x25, starting transfers between devices, shift(): lax.ppermute(value, axis, [(i, (i + step) % count) for i in range(count)])  59.6 us
    all_to_all x1, waiting for transfers between devices, reduce_features(): parts = lax.all_to_all(pair, CHIPS, 0, 0, tiled=True)  39 us
    all_gather x1, waiting for transfers between devices, local(): conv_weight = lax.all_gather(conv_out_weight, SEQ, axis=0, tiled=True)  29.2 us
    all_to_all x1, blocking collectives, reduce_features(): parts = lax.all_to_all(pair, CHIPS, 0, 0, tiled=True)  21.2 us
    pallas_call x6, Pallas kernels, run_kernel(): pl.pallas_call(body, out_shape=outs, in_specs=[smem()] + [vmem()] * len(a...  18 us
    all_to_all x1, blocking collectives, gather_features(): lax.all_to_all(jnp.broadcast_to(value, (8,) + value.shape), CHIPS, 0, 0,...  17.6 us
    all_to_all x1, starting transfers between devices, reduce_features(): parts = lax.all_to_all(pair, CHIPS, 0, 0, tiled=True)  9.45 us
  transfers between devices with their start and end apart: 29, of which 20 were waited for; matrix products, arithmetic and copies ran while one was open for 1% of the time, Pallas kernels for 5%

profile of v1, /device:TPU:1, one launch (start us, length us, event | category | flops | bytes accessed | tf_op | source)
XLA Modules:
  0.0 314.9 jit_solution(922624525904988430)
XLA Ops:
  10.6 4.0 %collective-permute-start.1 = (bf16[3,256,256]{2,1,0:T(8,128)(2,1)}, bf16[3,256,256]{2,1,0:T(8,128)(2,1)S(1)}, u32[]{:S(2)}, u32[]{:S(2)}) collective-permute-start(bf16[3,256,256]{2,1,0:T(8,128)(2,1)} %refs_0_.1), channel_id=1, source_target_pairs={{0,224},{32,0},{64,32},{96,64},{128,96},{160,128},{192,160},{224,1... | collective-permute-start | bytes 1179656 | tf_op jit(solution)/shard_map/ppermute | solution.py:18
  26.3 8.0 %collective-permute-done.5.refs_7_ = bf16[3,256,256]{2,1,0:T(8,128)(2,1)S(1)} collective-permute-done((bf16[3,256,256]{2,1,0:T(8,128)(2,1)S(1)}, bf16[3,256,256]{2,1,0:T(8,128)(2,1)S(1)}, u32[]{:S(2)}, u32[]{:S(2)}) %collective-permute-start.5) | collective-permute-done | bytes 393248 | tf_op jit(solution)/shard_map/ppermute | solution.py:18
  34.3 3.9 %collective-permute-done.2.refs_2_ = bf16[3,256,256]{2,1,0:T(8,128)(2,1)S(1)} collective-permute-done((bf16[3,256,256]{2,1,0:T(8,128)(2,1)S(1)}, bf16[3,256,256]{2,1,0:T(8,128)(2,1)S(1)}, u32[]{:S(2)}, u32[]{:S(2)}) %collective-permute-start.2) | collective-permute-done | bytes 393248 | tf_op jit(solution)/shard_map/ppermute | solution.py:18
  38.3 5.8 %collective-permute-done.6.refs_6_ = bf16[3,256,256]{2,1,0:T(8,128)(2,1)S(1)} collective-permute-done((bf16[3,256,256]{2,1,0:T(8,128)(2,1)S(1)}, bf16[3,256,256]{2,1,0:T(8,128)(2,1)S(1)}, u32[]{:S(2)}, u32[]{:S(2)}) %collective-permute-start.6) | collective-permute-done | bytes 393248 | tf_op jit(solution)/shard_map/ppermute | solution.py:18
  44.3 7.3 %collective-permute-done.3.refs_3_ = bf16[3,256,256]{2,1,0:T(8,128)(2,1)S(1)} collective-permute-done((bf16[3,256,256]{2,1,0:T(8,128)(2,1)S(1)}, bf16[3,256,256]{2,1,0:T(8,128)(2,1)S(1)}, u32[]{:S(2)}, u32[]{:S(2)}) %collective-permute-start.3) | collective-permute-done | bytes 393248 | tf_op jit(solution)/shard_map/ppermute | solution.py:18
  51.6 24.1 %collective-permute-done.got = bf16[8,256,256]{2,1,0:T(8,128)(2,1)S(1)} collective-permute-done((bf16[8,256,256]{2,1,0:T(8,128)(2,1)S(1)}, bf16[8,256,256]{2,1,0:T(8,128)(2,1)S(1)}, u32[]{:S(2)}, u32[]{:S(2)}) %collective-permute-start) | collective-permute-done | bytes 1048608 | tf_op jit(solution)/shard_map/ppermute | solution.py:18
  78.3 3.2 %collective-permute-start.10 = (bf16[2,2,256,128]{3,2,1,0:T(8,128)(2,1)S(1)}, bf16[2,2,256,128]{3,2,1,0:T(8,128)(2,1)S(1)}, u32[]{:S(2)}, u32[]{:S(2)}) collective-permute-start(bf16[2,2,256,128]{3,2,1,0:T(8,128)(2,1)S(1)} %slice.73), channel_id=1, source_target_pairs={{0,16},{16,0},{1,17},{17,1},{2,18},{18,2},{3,19},{19,3},{4,20},{20... | collective-permute-start | bytes 786440 | tf_op jit(solution)/shard_map/ppermute | solution.py:18
  81.6 8.9 %collective-permute-done.10 = bf16[2,2,256,128]{3,2,1,0:T(8,128)(2,1)S(1)} collective-permute-done((bf16[2,2,256,128]{3,2,1,0:T(8,128)(2,1)S(1)}, bf16[2,2,256,128]{3,2,1,0:T(8,128)(2,1)S(1)}, u32[]{:S(2)}, u32[]{:S(2)}) %collective-permute-start.10) | collective-permute-done | bytes 262176 | tf_op jit(solution)/shard_map/ppermute | solution.py:18
  100.1 3.4 %collective-permute-done.15 = bf16[2,2,256,128]{3,2,1,0:T(8,128)(2,1)S(1)} collective-permute-done((bf16[2,2,256,128]{3,2,1,0:T(8,128)(2,1)S(1)}, bf16[2,2,256,128]{3,2,1,0:T(8,128)(2,1)S(1)}, u32[]{:S(2)}, u32[]{:S(2)}) %collective-permute-start.15) | collective-permute-done | bytes 262176 | tf_op jit(solution)/shard_map/ppermute | solution.py:18
  106.8 4.6 %collective-permute-done.16 = bf16[2,2,256,128]{3,2,1,0:T(8,128)(2,1)S(1)} collective-permute-done((bf16[2,2,256,128]{3,2,1,0:T(8,128)(2,1)S(1)}, bf16[2,2,256,128]{3,2,1,0:T(8,128)(2,1)S(1)}, u32[]{:S(2)}, u32[]{:S(2)}) %collective-permute-start.16) | collective-permute-done | bytes 262176 | tf_op jit(solution)/shard_map/ppermute | solution.py:18
  111.5 4.7 %collective-permute-done.13 = bf16[2,2,256,128]{3,2,1,0:T(8,128)(2,1)S(1)} collective-permute-done((bf16[2,2,256,128]{3,2,1,0:T(8,128)(2,1)S(1)}, bf16[2,2,256,128]{3,2,1,0:T(8,128)(2,1)S(1)}, u32[]{:S(2)}, u32[]{:S(2)}) %collective-permute-start.13) | collective-permute-done | bytes 262176 | tf_op jit(solution)/shard_map/ppermute | solution.py:18
  118.3 6.2 %collective-permute-done.18 = bf16[1,2,256,128]{3,2,1,0:T(8,128)(2,1)S(1)} collective-permute-done((bf16[1,2,256,128]{3,2,1,0:T(8,128)(2,1)S(1)}, bf16[1,2,256,128]{3,2,1,0:T(8,128)(2,1)S(1)}, u32[]{:S(2)}, u32[]{:S(2)}) %collective-permute-start.18) | collective-permute-done | bytes 131104 | tf_op jit(solution)/shard_map/ppermute | solution.py:18
  124.5 4.8 %shard_map.102 = (bf16[256,128]{1,0:T(8,128)(2,1)S(1)}, bf16[256,128]{1,0:T(8,128)(2,1)S(1)}) custom-call(s32[4]{0:T(128)S(1)} %pad_add_fusion.where, f32[1,2,256,128]{3,2,1,0:T(8,128)S(1)} %slice.70.q_keep, bf16[1,2,256,128]{3,2,1,0:T(8,128)(2,1)S(1)} %collective-permute-done.9.q_got, bf16[2,256,128]{2,1,0:T(8,128)(2,1)S(1)} %get-tuple-element.40.refs_0_, ...), custom_call_target="tpu_custom_call" | custom-call | flops 1073741824 | bytes 4194304 | tf_op jit(solution)/shard_map/pallas_call | solution.py:30
  130.9 4.7 %collective-permute-done.19.got = bf16[256,128]{1,0:T(8,128)(2,1)S(1)} collective-permute-done((bf16[256,128]{1,0:T(8,128)(2,1)S(1)}, bf16[256,128]{1,0:T(8,128)(2,1)S(1)}, u32[]{:S(2)}, u32[]{:S(2)}) %collective-permute-start.19) | collective-permute-done | bytes 65568 | tf_op jit(solution)/shard_map/ppermute | solution.py:18
  138.4 12.2 %collective-permute-start.20 = (bf16[8,256,256]{2,1,0:T(8,128)(2,1)S(1)}, bf16[8,256,256]{2,1,0:T(8,128)(2,1)S(1)}, u32[]{:S(2)}, u32[]{:S(2)}) collective-permute-start(bf16[8,256,256]{2,1,0:T(8,128)(2,1)S(1)} %get-tuple-element.22), channel_id=1, source_target_pairs={{0,1},{1,0},{2,3},{3,2},{4,5},{5,4},{6,7},{7,6},{8,9},{9,8},{10,11... | collective-permute-start | bytes 3145736 | tf_op jit(solution)/shard_map/ppermute | solution.py:18
  154.2 9.4 %all-to-all-start = ((bf16[8,256,256]{2,1,0:T(8,128)(2,1)}), bf16[8,256,256]{2,1,0:T(8,128)(2,1)S(1)}, u32[]{:S(2)}, u32[]{:S(2)}) async-start(bf16[8,256,256]{2,1,0:T(8,128)(2,1)} %add_convert_fusion.1), calls=%async_computation | async-start | bytes 2097152 | tf_op jit(solution)/shard_map/all_to_all | solution.py:195
  163.7 39.0 %all-to-all-done = bf16[8,256,256]{2,1,0:T(8,128)(2,1)S(1)} async-done(((bf16[8,256,256]{2,1,0:T(8,128)(2,1)}), bf16[8,256,256]{2,1,0:T(8,128)(2,1)S(1)}, u32[]{:S(2)}, u32[]{:S(2)}) %all-to-all-start) | async-done | bytes 1048608 | tf_op jit(solution)/shard_map/all_to_all | solution.py:195
  203.9 17.6 %all_to_all.15.mine = bf16[8,256,256]{2,1,0:T(8,128)(2,1)S(1)} all-to-all(bf16[8,256,256]{2,1,0:T(8,128)(2,1)S(1)} %broadcast_in_dim.3), channel_id=1, replica_groups=mesh['z'=8,'xl'=2,'xh'=2,'y'=4,'c'=2] {'xh','y'}, dimensions={0} | all-to-all | bytes 2097152 | tf_op jit(solution)/shard_map/all_to_all | solution.py:200
  221.4 6.2 %collective-permute-start.21 = (bf16[8,256,256]{2,1,0:T(8,128)(2,1)S(1)}, bf16[8,256,256]{2,1,0:T(8,128)(2,1)S(1)}, u32[]{:S(2)}, u32[]{:S(2)}) collective-permute-start(bf16[8,256,256]{2,1,0:T(8,128)(2,1)S(1)} %all_to_all.15.mine), channel_id=1, source_target_pairs={{0,1},{1,0},{2,3},{3,2},{4,5},{5,4},{6,7},{7,6},{8,9},{9,8},{10,11... | collective-permute-start | bytes 3145736 | tf_op jit(solution)/shard_map/ppermute | solution.py:18
  232.1 4.0 %shard_map.104.gated = bf16[256,256]{1,0:T(8,128)(2,1)S(1)} custom-call(s32[4]{0:T(128)S(1)} %pad_add_fusion.where, bf16[8,256,256]{2,1,0:T(8,128)(2,1)S(1)} %all_to_all.15.mine, bf16[8,256,256]{2,1,0:T(8,128)(2,1)S(1)} %collective-permute-done.21.other, f32[1,4096]{1,0:T(1,128)S(1)} %bitcast.38, bf16[2,4096,256]{2,1,0:T(8,128)(2,1)S(1)} %copy-done), custom_call_target="tpu_custom_call" | custom-call | flops 1073741824 | bytes 6291456 | tf_op jit(solution)/shard_map/pallas_call | solution.py:30
  236.4 3.6 %collective-permute-start.23 = (bf16[16,256]{1,0:T(8,128)(2,1)S(1)}, bf16[16,256]{1,0:T(8,128)(2,1)S(1)}, u32[]{:S(2)}, u32[]{:S(2)}) collective-permute-start(bf16[16,256]{1,0:T(8,128)(2,1)S(1)} %get-tuple-element.41), channel_id=1, source_target_pairs={{0,240},{16,0},{32,16},{48,32},{64,48},{80,64},{96,80},{112,96},{1... | collective-permute-start | bytes 24584 | tf_op jit(solution)/shard_map/ppermute | solution.py:18
  240.0 29.2 %all-gather.8.cloned.1.call-done.weight = bf16[4096,256]{1,0:T(8,128)(2,1)} async-done(((bf16[256,256]{1,0:T(8,128)(2,1)}), bf16[4096,256]{1,0:T(8,128)(2,1)}) %all-gather.8.cloned.1.call-update) | async-done | bytes 2097168 | tf_op jit(solution)/shard_map/all_gather | solution.py:225
  273.3 10.4 %collective-permute-start.24 = (bf16[8,256,256]{2,1,0:T(8,128)(2,1)S(1)}, bf16[8,256,256]{2,1,0:T(8,128)(2,1)S(1)}, u32[]{:S(2)}, u32[]{:S(2)}) collective-permute-start(bf16[8,256,256]{2,1,0:T(8,128)(2,1)S(1)} %get-tuple-element.24), channel_id=1, source_target_pairs={{0,1},{1,0},{2,3},{3,2},{4,5},{5,4},{6,7},{7,6},{8,9},{9,8},{10,11... | collective-permute-start | bytes 3145736 | tf_op jit(solution)/shard_map/ppermute | solution.py:18
  286.3 21.2 %all_to_all.16 = bf16[8,256,256]{2,1,0:T(8,128)(2,1)S(1)} all-to-all(bf16[8,256,256]{2,1,0:T(8,128)(2,1)S(1)} %add_convert_fusion), channel_id=1, replica_groups=mesh['z'=8,'xl'=2,'xh'=2,'y'=4,'c'=2] {'xh','y'}, dimensions={0} | all-to-all | bytes 2097152 | tf_op jit(solution)/shard_map/all_to_all | solution.py:195
  (87 shorter events, 55.1 us)
Async XLA Ops:
  6.5 129.0 %all-gather.4.cloned.1.call-start = ((), (), s32[]{:S(2)}) async-start(), calls=%async_computation.3 | async-start | bytes 2228224 | tf_op jit(solution)/shard_map/all_gather | solution.py:223
  7.3 222.6 %all-gather.6.cloned.1.call-start = ((), (), s32[]{:S(2)}) async-start(), calls=%async_computation.4 | async-start | bytes 4456448 | tf_op jit(solution)/shard_map/all_gather | solution.py:224
  8.0 261.2 %all-gather.8.cloned.1.call-start = ((), (), s32[]{:S(2)}) async-start(), calls=%async_computation.5 | async-start | bytes 2228224 | tf_op jit(solution)/shard_map/all_gather | solution.py:225
  8.1 15.5 %collective-permute-start.4 = (bf16[3,256,256]{2,1,0:T(8,128)(2,1)}, bf16[3,256,256]{2,1,0:T(8,128)(2,1)S(1)}, u32[]{:S(2)}, u32[]{:S(2)}) collective-permute-start(bf16[3,256,256]{2,1,0:T(8,128)(2,1)} %refs_0_.1), channel_id=1, source_target_pairs={{0,32},{32,64},{64,96},{96,128},{128,160},{160,192},{192,224},{224... | collective-permute-start | bytes 1179656 | tf_op jit(solution)/shard_map/ppermute | solution.py:18
  10.6 13.0 %collective-permute-start.1 = (bf16[3,256,256]{2,1,0:T(8,128)(2,1)}, bf16[3,256,256]{2,1,0:T(8,128)(2,1)S(1)}, u32[]{:S(2)}, u32[]{:S(2)}) collective-permute-start(bf16[3,256,256]{2,1,0:T(8,128)(2,1)} %refs_0_.1), channel_id=1, source_target_pairs={{0,224},{32,0},{64,32},{96,64},{128,96},{160,128},{192,160},{224,1... | collective-permute-start | bytes 1179656 | tf_op jit(solution)/shard_map/ppermute | solution.py:18
  19.9 55.8 %collective-permute-start = (bf16[8,256,256]{2,1,0:T(8,128)(2,1)S(1)}, bf16[8,256,256]{2,1,0:T(8,128)(2,1)S(1)}, u32[]{:S(2)}, u32[]{:S(2)}) collective-permute-start(bf16[8,256,256]{2,1,0:T(8,128)(2,1)S(1)} %get-tuple-element.16), channel_id=1, source_target_pairs={{0,16},{16,0},{1,17},{17,1},{2,18},{18,2},{3,19},{19,3},{4,20},{20... | collective-permute-start | bytes 3145736 | tf_op jit(solution)/shard_map/ppermute | solution.py:18
  23.6 10.7 %collective-permute-start.5 = (bf16[3,256,256]{2,1,0:T(8,128)(2,1)S(1)}, bf16[3,256,256]{2,1,0:T(8,128)(2,1)S(1)}, u32[]{:S(2)}, u32[]{:S(2)}) collective-permute-start(bf16[3,256,256]{2,1,0:T(8,128)(2,1)S(1)} %collective-permute-done.4.refs_8_), channel_id=1, source_target_pairs={{0,32},{32,64},{64,96},{96,128},{128,160},{160,192},{192,224},{224... | collective-permute-start | bytes 1179656 | tf_op jit(solution)/shard_map/ppermute | solution.py:18
  23.6 14.6 %collective-permute-start.2 = (bf16[3,256,256]{2,1,0:T(8,128)(2,1)S(1)}, bf16[3,256,256]{2,1,0:T(8,128)(2,1)S(1)}, u32[]{:S(2)}, u32[]{:S(2)}) collective-permute-start(bf16[3,256,256]{2,1,0:T(8,128)(2,1)S(1)} %collective-permute-done.1.refs_1_), channel_id=1, source_target_pairs={{0,224},{32,0},{64,32},{96,64},{128,96},{160,128},{192,160},{224,1... | collective-permute-start | bytes 1179656 | tf_op jit(solution)/shard_map/ppermute | solution.py:18
  34.3 9.9 %collective-permute-start.6 = (bf16[3,256,256]{2,1,0:T(8,128)(2,1)S(1)}, bf16[3,256,256]{2,1,0:T(8,128)(2,1)S(1)}, u32[]{:S(2)}, u32[]{:S(2)}) collective-permute-start(bf16[3,256,256]{2,1,0:T(8,128)(2,1)S(1)} %collective-permute-done.5.refs_7_), channel_id=1, source_target_pairs={{0,32},{32,64},{64,96},{96,128},{128,160},{160,192},{192,224},{224... | collective-permute-start | bytes 1179656 | tf_op jit(solution)/shard_map/ppermute | solution.py:18
  38.2 13.3 %collective-permute-start.3 = (bf16[3,256,256]{2,1,0:T(8,128)(2,1)S(1)}, bf16[3,256,256]{2,1,0:T(8,128)(2,1)S(1)}, u32[]{:S(2)}, u32[]{:S(2)}) collective-permute-start(bf16[3,256,256]{2,1,0:T(8,128)(2,1)S(1)} %collective-permute-done.2.refs_2_), channel_id=1, source_target_pairs={{0,224},{32,0},{64,32},{96,64},{128,96},{160,128},{192,160},{224,1... | collective-permute-start | bytes 1179656 | tf_op jit(solution)/shard_map/ppermute | solution.py:18
  44.2 31.6 %collective-permute-start.7 = (bf16[3,128,256]{2,1,0:T(8,128)(2,1)S(1)}, bf16[3,128,256]{2,1,0:T(8,128)(2,1)S(1)}, u32[]{:S(2)}, u32[]{:S(2)}) collective-permute-start(bf16[3,128,256]{2,1,0:T(8,128)(2,1)S(1)} %slice.90), channel_id=1, source_target_pairs={{0,32},{32,64},{64,96},{96,128},{128,160},{160,192},{192,224},{224... | collective-permute-start | bytes 589832 | tf_op jit(solution)/shard_map/ppermute | solution.py:18
  51.5 24.2 %collective-permute-start.8 = (bf16[3,128,256]{2,1,0:T(8,128)(2,1)S(1)}, bf16[3,128,256]{2,1,0:T(8,128)(2,1)S(1)}, u32[]{:S(2)}, u32[]{:S(2)}) collective-permute-start(bf16[3,128,256]{2,1,0:T(8,128)(2,1)S(1)} %slice.91), channel_id=1, source_target_pairs={{0,224},{32,0},{64,32},{96,64},{128,96},{160,128},{192,160},{224,1... | collective-permute-start | bytes 589832 | tf_op jit(solution)/shard_map/ppermute | solution.py:18
  78.3 12.2 %collective-permute-start.10 = (bf16[2,2,256,128]{3,2,1,0:T(8,128)(2,1)S(1)}, bf16[2,2,256,128]{3,2,1,0:T(8,128)(2,1)S(1)}, u32[]{:S(2)}, u32[]{:S(2)}) collective-permute-start(bf16[2,2,256,128]{3,2,1,0:T(8,128)(2,1)S(1)} %slice.73), channel_id=1, source_target_pairs={{0,16},{16,0},{1,17},{17,1},{2,18},{18,2},{3,19},{19,3},{4,20},{20... | collective-permute-start | bytes 786440 | tf_op jit(solution)/shard_map/ppermute | solution.py:18
  93.4 24.2 %collective-permute-start.9 = (bf16[1,2,256,128]{3,2,1,0:T(8,128)(2,1)S(1)}, bf16[1,2,256,128]{3,2,1,0:T(8,128)(2,1)S(1)}, u32[]{:S(2)}, u32[]{:S(2)}) collective-permute-start(bf16[1,2,256,128]{3,2,1,0:T(8,128)(2,1)S(1)} %slice.71), channel_id=1, source_target_pairs={{0,16},{16,0},{1,17},{17,1},{2,18},{18,2},{3,19},{19,3},{4,20},{20... | collective-permute-start | bytes 393224 | tf_op jit(solution)/shard_map/ppermute | solution.py:18
  103.5 7.9 %collective-permute-start.16 = (bf16[2,2,256,128]{3,2,1,0:T(8,128)(2,1)S(1)}, bf16[2,2,256,128]{3,2,1,0:T(8,128)(2,1)S(1)}, u32[]{:S(2)}, u32[]{:S(2)}) collective-permute-start(bf16[2,2,256,128]{3,2,1,0:T(8,128)(2,1)S(1)} %collective-permute-done.15), channel_id=1, source_target_pairs={{0,32},{32,64},{64,96},{96,128},{128,160},{160,192},{192,224},{224... | collective-permute-start | bytes 786440 | tf_op jit(solution)/shard_map/ppermute | solution.py:18
  103.6 12.5 %collective-permute-start.13 = (bf16[2,2,256,128]{3,2,1,0:T(8,128)(2,1)S(1)}, bf16[2,2,256,128]{3,2,1,0:T(8,128)(2,1)S(1)}, u32[]{:S(2)}, u32[]{:S(2)}) collective-permute-start(bf16[2,2,256,128]{3,2,1,0:T(8,128)(2,1)S(1)} %collective-permute-done.12), channel_id=1, source_target_pairs={{0,224},{32,0},{64,32},{96,64},{128,96},{160,128},{192,160},{224,1... | collective-permute-start | bytes 786440 | tf_op jit(solution)/shard_map/ppermute | solution.py:18
  111.4 6.9 %collective-permute-start.17 = (bf16[1,2,256,128]{3,2,1,0:T(8,128)(2,1)S(1)}, bf16[1,2,256,128]{3,2,1,0:T(8,128)(2,1)S(1)}, u32[]{:S(2)}, u32[]{:S(2)}) collective-permute-start(bf16[1,2,256,128]{3,2,1,0:T(8,128)(2,1)S(1)} %get-tuple-element.31), channel_id=1, source_target_pairs={{0,32},{32,64},{64,96},{96,128},{128,160},{160,192},{192,224},{224... | collective-permute-start | bytes 393224 | tf_op jit(solution)/shard_map/ppermute | solution.py:18
  116.2 8.3 %collective-permute-start.18 = (bf16[1,2,256,128]{3,2,1,0:T(8,128)(2,1)S(1)}, bf16[1,2,256,128]{3,2,1,0:T(8,128)(2,1)S(1)}, u32[]{:S(2)}, u32[]{:S(2)}) collective-permute-start(bf16[1,2,256,128]{3,2,1,0:T(8,128)(2,1)S(1)} %get-tuple-element.32), channel_id=1, source_target_pairs={{0,224},{32,0},{64,32},{96,64},{128,96},{160,128},{192,160},{224,1... | collective-permute-start | bytes 393224 | tf_op jit(solution)/shard_map/ppermute | solution.py:18
  138.4 14.5 %collective-permute-start.20 = (bf16[8,256,256]{2,1,0:T(8,128)(2,1)S(1)}, bf16[8,256,256]{2,1,0:T(8,128)(2,1)S(1)}, u32[]{:S(2)}, u32[]{:S(2)}) collective-permute-start(bf16[8,256,256]{2,1,0:T(8,128)(2,1)S(1)} %get-tuple-element.22), channel_id=1, source_target_pairs={{0,1},{1,0},{2,3},{3,2},{4,5},{5,4},{6,7},{7,6},{8,9},{9,8},{10,11... | collective-permute-start | bytes 3145736 | tf_op jit(solution)/shard_map/ppermute | solution.py:18
  154.2 48.5 %all-to-all-start = ((bf16[8,256,256]{2,1,0:T(8,128)(2,1)}), bf16[8,256,256]{2,1,0:T(8,128)(2,1)S(1)}, u32[]{:S(2)}, u32[]{:S(2)}) async-start(bf16[8,256,256]{2,1,0:T(8,128)(2,1)} %add_convert_fusion.1), calls=%async_computation | async-start | bytes 2097152 | tf_op jit(solution)/shard_map/all_to_all | solution.py:195
  221.4 8.5 %collective-permute-start.21 = (bf16[8,256,256]{2,1,0:T(8,128)(2,1)S(1)}, bf16[8,256,256]{2,1,0:T(8,128)(2,1)S(1)}, u32[]{:S(2)}, u32[]{:S(2)}) collective-permute-start(bf16[8,256,256]{2,1,0:T(8,128)(2,1)S(1)} %all_to_all.15.mine), channel_id=1, source_target_pairs={{0,1},{1,0},{2,3},{3,2},{4,5},{5,4},{6,7},{7,6},{8,9},{9,8},{10,11... | collective-permute-start | bytes 3145736 | tf_op jit(solution)/shard_map/ppermute | solution.py:18
  236.1 33.1 %collective-permute-start.22 = (bf16[16,256]{1,0:T(8,128)(2,1)S(1)}, bf16[16,256]{1,0:T(8,128)(2,1)S(1)}, u32[]{:S(2)}, u32[]{:S(2)}) collective-permute-start(bf16[16,256]{1,0:T(8,128)(2,1)S(1)} %get-tuple-element.42), channel_id=1, source_target_pairs={{0,16},{16,32},{32,48},{48,64},{64,80},{80,96},{96,112},{112,128},... | collective-permute-start | bytes 24584 | tf_op jit(solution)/shard_map/ppermute | solution.py:18
  236.4 32.8 %collective-permute-start.23 = (bf16[16,256]{1,0:T(8,128)(2,1)S(1)}, bf16[16,256]{1,0:T(8,128)(2,1)S(1)}, u32[]{:S(2)}, u32[]{:S(2)}) collective-permute-start(bf16[16,256]{1,0:T(8,128)(2,1)S(1)} %get-tuple-element.41), channel_id=1, source_target_pairs={{0,240},{16,0},{32,16},{48,32},{64,48},{80,64},{96,80},{112,96},{1... | collective-permute-start | bytes 24584 | tf_op jit(solution)/shard_map/ppermute | solution.py:18
  273.3 12.7 %collective-permute-start.24 = (bf16[8,256,256]{2,1,0:T(8,128)(2,1)S(1)}, bf16[8,256,256]{2,1,0:T(8,128)(2,1)S(1)}, u32[]{:S(2)}, u32[]{:S(2)}) collective-permute-start(bf16[8,256,256]{2,1,0:T(8,128)(2,1)S(1)} %get-tuple-element.24), channel_id=1, source_target_pairs={{0,1},{1,0},{2,3},{3,2},{4,5},{5,4},{6,7},{7,6},{8,9},{9,8},{10,11... | collective-permute-start | bytes 3145736 | tf_op jit(solution)/shard_map/ppermute | solution.py:18
  (15 other events, 247.5 us)
Sparse Core Ops, SparseCore 0:
  9.1 79.9 all-gather.3
  91.0 112.7 all-gather.5
  205.6 63.5 all-gather.7

commit v2 on v1

--- a/solution.py
+++ b/solution.py
@@ -50,7 +50,7 @@
     rows, width = frames.shape
     blocks = mine.shape[0]
     block = mine.shape[2]
-    z, xl = where[0], where[1]
+    z, xl, core = where[0], where[1], where[2]
     step_rows = 32
 
     def chunk(i, carry):
@@ -59,10 +59,10 @@
         mean = jnp.mean(wide, axis=-1, keepdims=True)
         centered = wide - mean
         scale = lax.rsqrt(jnp.mean(centered * centered, axis=-1, keepdims=True) + 1e-05)
-        for j in range(blocks):
-            owner = lax.rem(z + j, blocks) * 2
-            for out, parity in ((mine, xl), (other, 1 - xl)):
-                cols = pl.ds(pl.multiple_of((owner + parity) * block, block), block)
+        for out, first, parity in ((mine, 0, xl), (other, core * other.shape[0], 1 - xl)):
+            for j in range(out.shape[0]):
+                owner = lax.rem(z + first + j, blocks) * 2 + parity
+                cols = pl.ds(pl.multiple_of(owner * block, block), block)
                 part = (frames[r, cols].astype(F32) - mean) * scale * gain[:, cols]
                 out[j, r, :] = part.astype(BF16)
         return carry
@@ -70,11 +70,13 @@
     lax.fori_loop(0, rows // step_rows, chunk, 0)
 
 
-def project_kernel(where, mine, got, *refs):
+def project_kernel(where, mine, got, swapped, *refs):
     pieces, (keep, send) = refs[:-2], refs[-2:]
-    xl = where[1]
+    xl, core = where[1], where[2]
+    low = [jnp.where(core == 0, got[j], swapped[j]) for j in range(4)]
+    high = [jnp.where(core == 0, swapped[j], got[j]) for j in range(4)]
     for m in range(3):
-        for r, a in enumerate((mine, got)):
+        for r, a in enumerate((mine, low + high)):
             acc = None
             for j in range(8):
                 if j < 4:
@@ -85,9 +87,9 @@
                 else:
                     term = dot(a[j], pieces[j + 1][m])
                 acc = term if acc is None else acc + term
-            low, high = acc[:, :HEAD_DIM], acc[:, HEAD_DIM:]
-            keep[m, r] = jnp.where(xl == 0, low, high)
-            send[m, r] = jnp.where(xl == 0, high, low).astype(BF16)
+            even, odd = acc[:, :HEAD_DIM], acc[:, HEAD_DIM:]
+            keep[m, r] = jnp.where(xl == 0, even, odd)
+            send[m, r] = jnp.where(xl == 0, odd, even).astype(BF16)
 
 
 def attend_kernel(where, q_keep, q_got, *refs):
@@ -114,35 +116,41 @@
             out[i : i + step_rows, :] = (acc / total).astype(BF16)
 
 
-def spread_out(inputs, weight, mine, other, core):
+def spread_out(inputs, weight, far_weight, mine, other, same):
     blocks, rows, block = mine.shape
     for j in range(blocks):
-        for out, parity in ((mine, core), (other, 1 - core)):
-            at = pl.ds(pl.multiple_of((2 * j + parity) * block, block), block)
-            out[j] = dot_t(inputs, weight[at, :]).astype(BF16)
-
-
-def project_out_kernel(where, own, got, weight, mine, other):
+        at = slice(j * block, (j + 1) * block)
+        a = dot_t(inputs, weight[at, :]).astype(BF16)
+        b = dot_t(inputs, far_weight[at, :]).astype(BF16)
+        mine[j] = jnp.where(same, a, b)
+        other[j] = jnp.where(same, b, a)
+
+
+def project_out_kernel(where, own, got, weight, far_weight, mine, other):
     xl = where[1]
     a, b = own[...], got[...]
     heads = jnp.concatenate([jnp.where(xl == 0, a, b), jnp.where(xl == 0, b, a)], axis=1)
-    spread_out(heads, weight, mine, other, where[2])
-
-
-def glu_kernel(where, mine, other, gain, weight, gated, normed):
+    spread_out(heads, weight, far_weight, mine, other, where[2] == xl)
+
+
+def glu_kernel(where, mine, other, gain, weight, far_weight, gated, normed):
     blocks, rows, block = mine.shape
-    core = where[2]
+    xl = where[1]
+    same = where[2] == xl
     step_rows = 32
     width = 2 * blocks * block
 
     def chunk(i, carry):
         r = pl.ds(pl.multiple_of(i * step_rows, step_rows), step_rows)
-        parts = [ref[j, r, :].astype(F32) for j in range(blocks) for ref in (mine, other)]
+        parts = []
+        for j in range(blocks):
+            a, b = mine[j, r, :], other[j, r, :]
+            parts += [jnp.where(same, a, b).astype(F32), jnp.where(same, b, a).astype(F32)]
         mean = jnp.sum(sum(parts), axis=-1, keepdims=True) / width
         square = sum((p - mean) * (p - mean) for p in parts)
         scale = lax.rsqrt(jnp.sum(square, axis=-1, keepdims=True) / width + 1e-05)
         for n, p in enumerate(parts):
-            parity = core if n % 2 == 0 else 1 - core
+            parity = xl if n % 2 == 0 else 1 - xl
             cols = pl.ds(pl.multiple_of((n // 2 * 2 + parity) * block, block), block)
             normed[n, r, :] = ((p - mean) * scale * gain[:, cols]).astype(BF16)
         return carry
@@ -150,15 +158,14 @@
     lax.fori_loop(0, rows // step_rows, chunk, 0)
     sums = [None, None]
     for n in range(2 * blocks):
-        parity = core if n % 2 == 0 else 1 - core
-        at = pl.ds(pl.multiple_of((n // 2 * 2 + parity) * block, block), block)
+        source = (weight, far_weight)[n % 2]
         for m in range(2):
-            term = dot(normed[n], weight[m, at, :])
+            term = dot(normed[n], source[m, n // 2 * block : (n // 2 + 1) * block, :])
             sums[m] = term if sums[m] is None else sums[m] + term
     gated[...] = (sums[0] * jax.nn.sigmoid(sums[1])).astype(BF16)
 
 
-def conv_kernel(where, gated, before, after, taps, scale, offset, weight, mine, other, padded, activated):
+def conv_kernel(where, gated, before, after, taps, scale, offset, weight, far_weight, mine, other, padded, activated):
     rows = gated.shape[0]
     rim = before.shape[0]
     seq = where[0] * 2 + where[1]
@@ -174,7 +181,7 @@
             acc = term if acc is None else acc + term
         v = acc * scale[...] + offset[...]
         activated[i : i + 32, :] = (v * jax.nn.sigmoid(v)).astype(BF16)
-    spread_out(activated[...], weight, mine, other, where[2])
+    spread_out(activated[...], weight, far_weight, mine, other, where[2] == where[1])
 
 
 def ring(value, first_half, second_half):
@@ -220,18 +227,22 @@
     where = jnp.stack([z, xl, core, lax.axis_size(SEQ)]).astype(jnp.int32)
     S = jax.ShapeDtypeStruct
 
-    out_weight = lax.all_gather(attn_out_weight, SEQ, axis=0, tiled=True)
-    glu_full = lax.all_gather(glu_weight, SEQ, axis=1, tiled=True)
-    conv_weight = lax.all_gather(conv_out_weight, SEQ, axis=0, tiled=True)
+    out_weight = lax.all_gather(attn_out_weight, "z", axis=0, tiled=True)
+    out_weight = [out_weight, shift(out_weight, "xl", 1)]
+    glu_half = lax.all_gather(glu_weight, "z", axis=1, tiled=True)
+    glu_half = [glu_half, shift(glu_half, "xl", 1)]
+    conv_weight = lax.all_gather(conv_out_weight, "z", axis=0, tiled=True)
+    conv_weight = [conv_weight, shift(conv_weight, "xl", 1)]
 
     half = block // 2
     pieces = ring(qkv_weight, lambda v: v[:, :half], lambda v: v[:, half:])
     mine, other = run_kernel(
         norm_blocks_kernel, where, [frames, attn_norm_gain.reshape(1, width)],
-        [S((blocks, rows, block), BF16)] * 2, [], 16, 10 * rows * width, 4 * rows * width)
+        [S((blocks, rows, block), BF16), S((blocks // 2, rows, block), BF16)], [], 16, 10 * rows * width, 4 * rows * width)
     got = shift(other, "xl", 1)
+    swapped = shift(got, "c", 1)
     keep, send = run_kernel(
-        project_kernel, where, [mine, got] + pieces,
+        project_kernel, where, [mine, got, swapped] + pieces,
         [S((3, 2, rows, HEAD_DIM), F32), S((3, 2, rows, HEAD_DIM), BF16)], [], 24,
         6 * rows * width * block, 6 * block * block * 8 + 4 * rows * width)
     kv_got = shift(send[1:], "xl", 1)
@@ -251,13 +262,13 @@
     back = shift(away, "xl", 1)
     blocks_out = [S((blocks, rows, block), BF16)] * 2
     mine, other = run_kernel(
-        project_out_kernel, where, [own, back, out_weight], blocks_out, [], 16,
+        project_out_kernel, where, [own, back] + out_weight, blocks_out, [], 16,
         2 * rows * block * width, 4 << 20)
     frame_cols = lax.dynamic_slice_in_dim(frames, lax.axis_index(WT) * block, block, 1)
     mixed = (frame_cols.astype(F32) + reduce_features(mine, other)).astype(BF16)
     mine, other = gather_features(mixed)
     gated = run_kernel(
-        glu_kernel, where, [mine, other, conv_norm_gain.reshape(1, width), glu_full],
+        glu_kernel, where, [mine, other, conv_norm_gain.reshape(1, width)] + glu_half,
         S((rows, block), BF16), [pltpu.VMEM((2 * blocks, rows, block), BF16)], 24,
         4 * rows * block * width, 6 << 20)
     rim = 16
@@ -265,7 +276,7 @@
     after = shift(gated[:rim], SEQ, -1)
     mine, other = run_kernel(
         conv_kernel, where,
-        [gated, before, after, depth_kernel, norm_scale.reshape(1, block), norm_shift.reshape(1, block), conv_weight],
+        [gated, before, after, depth_kernel, norm_scale.reshape(1, block), norm_shift.reshape(1, block)] + conv_weight,
         blocks_out, [pltpu.VMEM((rows + 2 * rim, block), F32), pltpu.VMEM((rows, block), BF16)], 16,
         2 * rows * block * width, 4 << 20)
     return (mixed.astype(F32) + reduce_features(mine, other)).astype(BF16)

time: 315 us -> 267 us (0.85)
  waiting for transfers between devices: 164 us -> 83.9 us
  blocking collectives: 38.8 us -> 74.3 us
  local copies, waits for them, and re-layouts: 8.04 us -> 3.68 us
    all_to_all x1, blocking collectives: 17.6 us -> 56 us  [gather_features(): lax.all_to_all(jnp.broadcast_to(value, (8,) + value.shape), CHIPS, 0, 0,...]
    all_gather x3, waiting for transfers between devices: 29.2 us -> 0.04 us  [the longest x1 0.02 us: local(): out_weight = lax.all_gather(attn_out_weight, 'z', axis=0, tiled=True)]
    all_to_all x1, waiting for transfers between devices: 39 us -> 13.7 us  [reduce_features(): parts = lax.all_to_all(pair, CHIPS, 0, 0, tiled=True)]
    ppermute x25 -> x29, waiting for transfers between devices: 94.3 us -> 69.5 us  [shift(): lax.ppermute(value, axis, [(i, (i + step) % count) for i in range(count)])]
    unnamed x20 -> x24, local copies, waits for them, and re-layouts: 7.72 us -> 3.35 us
    all_to_all x1, starting transfers between devices: 9.45 us -> 6.06 us  [reduce_features(): parts = lax.all_to_all(pair, CHIPS, 0, 0, tiled=True)]
    ppermute x25 -> x29, starting transfers between devices: 59.6 us -> 61.2 us  [shift(): lax.ppermute(value, axis, [(i, (i + step) % count) for i in range(count)])]
  transfers between devices with their start and end apart: 29 -> 33, of which waited for: 20 -> 21; matrix products, arithmetic and copies ran while one was open for 1% -> 1% of each run, Pallas kernels for 5% -> 7%
where the time goes in v2:
time: 267 us
  waiting for transfers between devices  83.9 us (31%)
  blocking collectives  74.3 us (28%)
  starting transfers between devices  67.4 us (25%)
  Pallas kernels  20.2 us (8%)
  between operations  13.4 us (5%)
  other arithmetic  3.73 us (1%)
  local copies, waits for them, and re-layouts  3.68 us (1%)
    ppermute x29, waiting for transfers between devices, shift(): lax.ppermute(value, axis, [(i, (i + step) % count) for i in range(count)])  69.5 us
    ppermute x29, starting transfers between devices, shift(): lax.ppermute(value, axis, [(i, (i + step) % count) for i in range(count)])  61.2 us
    all_to_all x1, blocking collectives, gather_features(): lax.all_to_all(jnp.broadcast_to(value, (8,) + value.shape), CHIPS, 0, 0,...  56 us
    pallas_call x6, Pallas kernels, run_kernel(): pl.pallas_call(body, out_shape=outs, in_specs=[smem()] + [vmem()] * len(a...  20.2 us
    all_to_all x1, blocking collectives, reduce_features(): parts = lax.all_to_all(pair, CHIPS, 0, 0, tiled=True)  18.4 us
    all_to_all x1, waiting for transfers between devices, reduce_features(): parts = lax.all_to_all(pair, CHIPS, 0, 0, tiled=True)  13.7 us
    all_to_all x1, starting transfers between devices, reduce_features(): parts = lax.all_to_all(pair, CHIPS, 0, 0, tiled=True)  6.06 us
  transfers between devices with their start and end apart: 33, of which 21 were waited for; matrix products, arithmetic and copies ran while one was open for 1% of the time, Pallas kernels for 7%

profile of v2, /device:TPU:1, one launch (start us, length us, event | category | flops | bytes accessed | tf_op | source)
XLA Modules:
  0.0 266.6 jit_solution(11051653993551259471)
XLA Ops:
  9.0 3.9 %collective-permute-start.2 = (bf16[3,256,256]{2,1,0:T(8,128)(2,1)}, bf16[3,256,256]{2,1,0:T(8,128)(2,1)}, u32[]{:S(2)}, u32[]{:S(2)}) collective-permute-start(bf16[3,256,256]{2,1,0:T(8,128)(2,1)} %refs_0_.1), channel_id=1, source_target_pairs={{0,224},{32,0},{64,32},{96,64},{128,96},{160,128},{192,160},{224,1... | collective-permute-start | bytes 1179656 | tf_op jit(solution)/shard_map/ppermute | solution.py:18
  24.7 7.9 %collective-permute-done.6.refs_7_ = bf16[3,256,256]{2,1,0:T(8,128)(2,1)} collective-permute-done((bf16[3,256,256]{2,1,0:T(8,128)(2,1)S(1)}, bf16[3,256,256]{2,1,0:T(8,128)(2,1)}, u32[]{:S(2)}, u32[]{:S(2)}) %collective-permute-start.6) | collective-permute-done | bytes 393248 | tf_op jit(solution)/shard_map/ppermute | solution.py:18
  38.1 5.9 %collective-permute-done.7.refs_6_ = bf16[3,256,256]{2,1,0:T(8,128)(2,1)S(1)} collective-permute-done((bf16[3,256,256]{2,1,0:T(8,128)(2,1)}, bf16[3,256,256]{2,1,0:T(8,128)(2,1)S(1)}, u32[]{:S(2)}, u32[]{:S(2)}) %collective-permute-start.7) | collective-permute-done | bytes 393248 | tf_op jit(solution)/shard_map/ppermute | solution.py:18
  45.4 3.5 %collective-permute-start.9 = (bf16[3,128,256]{2,1,0:T(8,128)(2,1)S(1)}, bf16[3,128,256]{2,1,0:T(8,128)(2,1)S(1)}, u32[]{:S(2)}, u32[]{:S(2)}) collective-permute-start(bf16[3,128,256]{2,1,0:T(8,128)(2,1)S(1)} %slice.91), channel_id=1, source_target_pairs={{0,224},{32,0},{64,32},{96,64},{128,96},{160,128},{192,160},{224,1... | collective-permute-start | bytes 589832 | tf_op jit(solution)/shard_map/ppermute | solution.py:18
  48.8 3.1 %collective-permute-done.8.refs_4_ = bf16[3,128,256]{2,1,0:T(8,128)(2,1)S(1)} collective-permute-done((bf16[3,128,256]{2,1,0:T(8,128)(2,1)S(1)}, bf16[3,128,256]{2,1,0:T(8,128)(2,1)S(1)}, u32[]{:S(2)}, u32[]{:S(2)}) %collective-permute-start.8) | collective-permute-done | bytes 196640 | tf_op jit(solution)/shard_map/ppermute | solution.py:18
  53.5 3.2 %shard_map.101 = (f32[3,2,256,128]{3,2,1,0:T(8,128)S(1)}, bf16[3,2,256,128]{3,2,1,0:T(8,128)(2,1)S(1)}) custom-call(s32[4]{0:T(128)S(1)} %pad_add_fusion.where, bf16[8,256,256]{2,1,0:T(8,128)(2,1)S(1)} %get-tuple-element.15.mine, bf16[4,256,256]{2,1,0:T(8,128)(2,1)S(1)} %collective-permute-done.got, bf16[4,256,256]{2,1,0:T(8,128)(2,1)S(1)} %collective-permute-done.1.swapped, ...), custom_call_target="tpu_custom_call" | custom-call | flops 1610612736 | bytes 7340032 | tf_op jit(solution)/shard_map/pallas_call | solution.py:30
  58.0 4.5 %collective-permute-done.11 = bf16[2,2,256,128]{3,2,1,0:T(8,128)(2,1)S(1)} collective-permute-done((bf16[2,2,256,128]{3,2,1,0:T(8,128)(2,1)S(1)}, bf16[2,2,256,128]{3,2,1,0:T(8,128)(2,1)S(1)}, u32[]{:S(2)}, u32[]{:S(2)}) %collective-permute-start.11) | collective-permute-done | bytes 262176 | tf_op jit(solution)/shard_map/ppermute | solution.py:18
  62.6 3.3 %collective-permute-start.12 = (bf16[2,2,256,128]{3,2,1,0:T(8,128)(2,1)S(1)}, bf16[2,2,256,128]{3,2,1,0:T(8,128)(2,1)S(1)}, u32[]{:S(2)}, u32[]{:S(2)}) collective-permute-start(bf16[2,2,256,128]{3,2,1,0:T(8,128)(2,1)S(1)} %add_convert_fusion.2), channel_id=1, source_target_pairs={{0,224},{32,0},{64,32},{96,64},{128,96},{160,128},{192,160},{224,1... | collective-permute-start | bytes 786440 | tf_op jit(solution)/shard_map/ppermute | solution.py:18
  73.4 4.8 %collective-permute-done.16 = bf16[2,2,256,128]{3,2,1,0:T(8,128)(2,1)S(1)} collective-permute-done((bf16[2,2,256,128]{3,2,1,0:T(8,128)(2,1)S(1)}, bf16[2,2,256,128]{3,2,1,0:T(8,128)(2,1)S(1)}, u32[]{:S(2)}, u32[]{:S(2)}) %collective-permute-start.16) | collective-permute-done | bytes 262176 | tf_op jit(solution)/shard_map/ppermute | solution.py:18
  79.3 3.4 %collective-permute-start.14 = (bf16[2,2,256,128]{3,2,1,0:T(8,128)(2,1)S(1)}, bf16[2,2,256,128]{3,2,1,0:T(8,128)(2,1)S(1)}, u32[]{:S(2)}, u32[]{:S(2)}) collective-permute-start(bf16[2,2,256,128]{3,2,1,0:T(8,128)(2,1)S(1)} %collective-permute-done.13), channel_id=1, source_target_pairs={{0,224},{32,0},{64,32},{96,64},{128,96},{160,128},{192,160},{224,1... | collective-permute-start | bytes 786440 | tf_op jit(solution)/shard_map/ppermute | solution.py:18
  82.7 3.1 %collective-permute-done.17 = bf16[2,2,256,128]{3,2,1,0:T(8,128)(2,1)S(1)} collective-permute-done((bf16[2,2,256,128]{3,2,1,0:T(8,128)(2,1)S(1)}, bf16[2,2,256,128]{3,2,1,0:T(8,128)(2,1)S(1)}, u32[]{:S(2)}, u32[]{:S(2)}) %collective-permute-start.17) | collective-permute-done | bytes 262176 | tf_op jit(solution)/shard_map/ppermute | solution.py:18
  86.0 4.6 %collective-permute-done.14 = bf16[2,2,256,128]{3,2,1,0:T(8,128)(2,1)S(1)} collective-permute-done((bf16[2,2,256,128]{3,2,1,0:T(8,128)(2,1)S(1)}, bf16[2,2,256,128]{3,2,1,0:T(8,128)(2,1)S(1)}, u32[]{:S(2)}, u32[]{:S(2)}) %collective-permute-start.14) | collective-permute-done | bytes 262176 | tf_op jit(solution)/shard_map/ppermute | solution.py:18
  90.6 3.6 %collective-permute-start.19 = (bf16[1,2,256,128]{3,2,1,0:T(8,128)(2,1)S(1)}, bf16[1,2,256,128]{3,2,1,0:T(8,128)(2,1)S(1)}, u32[]{:S(2)}, u32[]{:S(2)}) collective-permute-start(bf16[1,2,256,128]{3,2,1,0:T(8,128)(2,1)S(1)} %get-tuple-element.32), channel_id=1, source_target_pairs={{0,224},{32,0},{64,32},{96,64},{128,96},{160,128},{192,160},{224,1... | collective-permute-start | bytes 393224 | tf_op jit(solution)/shard_map/ppermute | solution.py:18
  94.6 3.2 %collective-permute-done.19 = bf16[1,2,256,128]{3,2,1,0:T(8,128)(2,1)S(1)} collective-permute-done((bf16[1,2,256,128]{3,2,1,0:T(8,128)(2,1)S(1)}, bf16[1,2,256,128]{3,2,1,0:T(8,128)(2,1)S(1)}, u32[]{:S(2)}, u32[]{:S(2)}) %collective-permute-start.19) | collective-permute-done | bytes 131104 | tf_op jit(solution)/shard_map/ppermute | solution.py:18
  97.7 4.7 %shard_map.102 = (bf16[256,128]{1,0:T(8,128)(2,1)S(1)}, bf16[256,128]{1,0:T(8,128)(2,1)S(1)}) custom-call(s32[4]{0:T(128)S(1)} %pad_add_fusion.where, f32[1,2,256,128]{3,2,1,0:T(8,128)S(1)} %slice.70.q_keep, bf16[1,2,256,128]{3,2,1,0:T(8,128)(2,1)S(1)} %collective-permute-done.10.q_got, bf16[2,256,128]{2,1,0:T(8,128)(2,1)S(1)} %get-tuple-element.40.refs_0_, ...), custom_call_target="tpu_custom_call" | custom-call | flops 1073741824 | bytes 4194304 | tf_op jit(solution)/shard_map/pallas_call | solution.py:30
  102.5 3.4 %collective-permute-done.20.got = bf16[256,128]{1,0:T(8,128)(2,1)S(1)} collective-permute-done((bf16[256,128]{1,0:T(8,128)(2,1)S(1)}, bf16[256,128]{1,0:T(8,128)(2,1)S(1)}, u32[]{:S(2)}, u32[]{:S(2)}) %collective-permute-start.20) | collective-permute-done | bytes 65568 | tf_op jit(solution)/shard_map/ppermute | solution.py:18
  107.3 18.3 %collective-permute-start.22 = (bf16[8,256,256]{2,1,0:T(8,128)(2,1)S(1)}, bf16[8,256,256]{2,1,0:T(8,128)(2,1)S(1)}, u32[]{:S(2)}, u32[]{:S(2)}) collective-permute-start(bf16[8,256,256]{2,1,0:T(8,128)(2,1)S(1)} %get-tuple-element.22), channel_id=1, source_target_pairs={{0,1},{1,0},{2,3},{3,2},{4,5},{5,4},{6,7},{7,6},{8,9},{9,8},{10,11... | collective-permute-start | bytes 3145736 | tf_op jit(solution)/shard_map/ppermute | solution.py:18
  129.1 6.1 %all-to-all-start = ((bf16[8,256,256]{2,1,0:T(8,128)(2,1)}), bf16[8,256,256]{2,1,0:T(8,128)(2,1)S(1)}, u32[]{:S(2)}, u32[]{:S(2)}) async-start(bf16[8,256,256]{2,1,0:T(8,128)(2,1)} %add_convert_fusion.1), calls=%async_computation | async-start | bytes 2097152 | tf_op jit(solution)/shard_map/all_to_all | solution.py:202
  136.0 13.7 %all-to-all-done = bf16[8,256,256]{2,1,0:T(8,128)(2,1)S(1)} async-done(((bf16[8,256,256]{2,1,0:T(8,128)(2,1)}), bf16[8,256,256]{2,1,0:T(8,128)(2,1)S(1)}, u32[]{:S(2)}, u32[]{:S(2)}) %all-to-all-start) | async-done | bytes 1048608 | tf_op jit(solution)/shard_map/all_to_all | solution.py:202
  151.0 56.0 %all_to_all.15.mine = bf16[8,256,256]{2,1,0:T(8,128)(2,1)S(1)} all-to-all(bf16[8,256,256]{2,1,0:T(8,128)(2,1)S(1)} %broadcast_in_dim.3), channel_id=1, replica_groups=mesh['z'=8,'xl'=2,'xh'=2,'y'=4,'c'=2] {'xh','y'}, dimensions={0} | all-to-all | bytes 2097152 | tf_op jit(solution)/shard_map/all_to_all | solution.py:207
  211.9 5.5 %shard_map.104.gated = bf16[256,256]{1,0:T(8,128)(2,1)S(1)} custom-call(s32[4]{0:T(128)S(1)} %pad_add_fusion.where, bf16[8,256,256]{2,1,0:T(8,128)(2,1)S(1)} %all_to_all.15.mine, bf16[8,256,256]{2,1,0:T(8,128)(2,1)} %collective-permute-done.23.other, f32[1,4096]{1,0:T(1,128)S(1)} %bitcast.38, bf16[2,2048,256]{2,1,0:T(8,128)(2,1)S(1)} %copy-done.1, ...), custom_call_target="tpu_custom_call" | custom-call | flops 1073741824 | bytes 6291456 | tf_op jit(solution)/shard_map/pallas_call | solution.py:30
  217.5 3.6 %collective-permute-start.26 = (bf16[16,256]{1,0:T(8,128)(2,1)S(1)}, bf16[16,256]{1,0:T(8,128)(2,1)S(1)}, u32[]{:S(2)}, u32[]{:S(2)}) collective-permute-start(bf16[16,256]{1,0:T(8,128)(2,1)S(1)} %get-tuple-element.41), channel_id=1, source_target_pairs={{0,240},{16,0},{32,16},{48,32},{64,48},{80,64},{96,80},{112,96},{1... | collective-permute-start | bytes 24584 | tf_op jit(solution)/shard_map/ppermute | solution.py:18
  221.0 13.5 %collective-permute-done.27.far_weight = bf16[2048,256]{1,0:T(8,128)(2,1)S(1)} collective-permute-done((bf16[2048,256]{1,0:T(8,128)(2,1)}, bf16[2048,256]{1,0:T(8,128)(2,1)S(1)}, u32[]{:S(2)}, u32[]{:S(2)}) %collective-permute-start.27) | collective-permute-done | bytes 1048608 | tf_op jit(solution)/shard_map/ppermute | solution.py:18
  240.8 18.4 %all_to_all.16 = bf16[8,256,256]{2,1,0:T(8,128)(2,1)S(1)} all-to-all(bf16[8,256,256]{2,1,0:T(8,128)(2,1)S(1)} %add_convert_fusion), channel_id=1, replica_groups=mesh['z'=8,'xl'=2,'xh'=2,'y'=4,'c'=2] {'xh','y'}, dimensions={0} | all-to-all | bytes 2097152 | tf_op jit(solution)/shard_map/all_to_all | solution.py:202
  (99 shorter events, 52.2 us)
Async XLA Ops:
  6.5 63.1 %all-gather.4.cloned.1.call-start = ((), (), s32[]{:S(2)}) async-start(), calls=%async_computation.3 | async-start | bytes 1179648 | tf_op jit(solution)/shard_map/all_gather | solution.py:230
  6.5 15.5 %collective-permute-start.5 = (bf16[3,256,256]{2,1,0:T(8,128)(2,1)}, bf16[3,256,256]{2,1,0:T(8,128)(2,1)S(1)}, u32[]{:S(2)}, u32[]{:S(2)}) collective-permute-start(bf16[3,256,256]{2,1,0:T(8,128)(2,1)} %refs_0_.1), channel_id=1, source_target_pairs={{0,32},{32,64},{64,96},{96,128},{128,160},{160,192},{192,224},{224... | collective-permute-start | bytes 1179656 | tf_op jit(solution)/shard_map/ppermute | solution.py:18
  9.0 13.0 %collective-permute-start.2 = (bf16[3,256,256]{2,1,0:T(8,128)(2,1)}, bf16[3,256,256]{2,1,0:T(8,128)(2,1)}, u32[]{:S(2)}, u32[]{:S(2)}) collective-permute-start(bf16[3,256,256]{2,1,0:T(8,128)(2,1)} %refs_0_.1), channel_id=1, source_target_pairs={{0,224},{32,0},{64,32},{96,64},{128,96},{160,128},{192,160},{224,1... | collective-permute-start | bytes 1179656 | tf_op jit(solution)/shard_map/ppermute | solution.py:18
  18.2 17.1 %collective-permute-start = (bf16[4,256,256]{2,1,0:T(8,128)(2,1)S(1)}, bf16[4,256,256]{2,1,0:T(8,128)(2,1)S(1)}, u32[]{:S(2)}, u32[]{:S(2)}) collective-permute-start(bf16[4,256,256]{2,1,0:T(8,128)(2,1)S(1)} %get-tuple-element.16), channel_id=1, source_target_pairs={{0,16},{16,0},{1,17},{17,1},{2,18},{18,2},{3,19},{19,3},{4,20},{20... | collective-permute-start | bytes 1572872 | tf_op jit(solution)/shard_map/ppermute | solution.py:18
  22.0 10.7 %collective-permute-start.6 = (bf16[3,256,256]{2,1,0:T(8,128)(2,1)S(1)}, bf16[3,256,256]{2,1,0:T(8,128)(2,1)}, u32[]{:S(2)}, u32[]{:S(2)}) collective-permute-start(bf16[3,256,256]{2,1,0:T(8,128)(2,1)S(1)} %collective-permute-done.5.refs_8_), channel_id=1, source_target_pairs={{0,32},{32,64},{64,96},{96,128},{128,160},{160,192},{192,224},{224... | collective-permute-start | bytes 1179656 | tf_op jit(solution)/shard_map/ppermute | solution.py:18
  22.0 10.7 %collective-permute-start.3 = (bf16[3,256,256]{2,1,0:T(8,128)(2,1)}, bf16[3,256,256]{2,1,0:T(8,128)(2,1)}, u32[]{:S(2)}, u32[]{:S(2)}) collective-permute-start(bf16[3,256,256]{2,1,0:T(8,128)(2,1)} %collective-permute-done.2.refs_1_), channel_id=1, source_target_pairs={{0,224},{32,0},{64,32},{96,64},{128,96},{160,128},{192,160},{224,1... | collective-permute-start | bytes 1179656 | tf_op jit(solution)/shard_map/ppermute | solution.py:18
  24.7 111.2 %all-gather.6.cloned.1.call-start = ((), (), s32[]{:S(2)}) async-start(), calls=%async_computation.4 | async-start | bytes 2359296 | tf_op jit(solution)/shard_map/all_gather | solution.py:232
  32.7 11.3 %collective-permute-start.7 = (bf16[3,256,256]{2,1,0:T(8,128)(2,1)}, bf16[3,256,256]{2,1,0:T(8,128)(2,1)S(1)}, u32[]{:S(2)}, u32[]{:S(2)}) collective-permute-start(bf16[3,256,256]{2,1,0:T(8,128)(2,1)} %collective-permute-done.6.refs_7_), channel_id=1, source_target_pairs={{0,32},{32,64},{64,96},{96,128},{128,160},{160,192},{192,224},{224... | collective-permute-start | bytes 1179656 | tf_op jit(solution)/shard_map/ppermute | solution.py:18
  32.7 12.6 %collective-permute-start.4 = (bf16[3,256,256]{2,1,0:T(8,128)(2,1)}, bf16[3,256,256]{2,1,0:T(8,128)(2,1)S(1)}, u32[]{:S(2)}, u32[]{:S(2)}) collective-permute-start(bf16[3,256,256]{2,1,0:T(8,128)(2,1)} %collective-permute-done.3.refs_2_), channel_id=1, source_target_pairs={{0,224},{32,0},{64,32},{96,64},{128,96},{160,128},{192,160},{224,1... | collective-permute-start | bytes 1179656 | tf_op jit(solution)/shard_map/ppermute | solution.py:18
  35.4 13.5 %collective-permute-start.1 = (bf16[4,256,256]{2,1,0:T(8,128)(2,1)S(1)}, bf16[4,256,256]{2,1,0:T(8,128)(2,1)S(1)}, u32[]{:S(2)}, u32[]{:S(2)}) collective-permute-start(bf16[4,256,256]{2,1,0:T(8,128)(2,1)S(1)} %collective-permute-done.got), channel_id=1, source_target_pairs={{0,1},{1,0},{2,3},{3,2},{4,5},{5,4},{6,7},{7,6},{8,9},{9,8},{10,11... | collective-permute-start | bytes 1572872 | tf_op jit(solution)/shard_map/ppermute | solution.py:18
  62.6 8.1 %collective-permute-start.12 = (bf16[2,2,256,128]{3,2,1,0:T(8,128)(2,1)S(1)}, bf16[2,2,256,128]{3,2,1,0:T(8,128)(2,1)S(1)}, u32[]{:S(2)}, u32[]{:S(2)}) collective-permute-start(bf16[2,2,256,128]{3,2,1,0:T(8,128)(2,1)S(1)} %add_convert_fusion.2), channel_id=1, source_target_pairs={{0,224},{32,0},{64,32},{96,64},{128,96},{160,128},{192,160},{224,1... | collective-permute-start | bytes 786440 | tf_op jit(solution)/shard_map/ppermute | solution.py:18
  66.0 28.2 %collective-permute-start.10 = (bf16[1,2,256,128]{3,2,1,0:T(8,128)(2,1)S(1)}, bf16[1,2,256,128]{3,2,1,0:T(8,128)(2,1)S(1)}, u32[]{:S(2)}, u32[]{:S(2)}) collective-permute-start(bf16[1,2,256,128]{3,2,1,0:T(8,128)(2,1)S(1)} %slice.71), channel_id=1, source_target_pairs={{0,16},{16,0},{1,17},{17,1},{2,18},{18,2},{3,19},{19,3},{4,20},{20... | collective-permute-start | bytes 393224 | tf_op jit(solution)/shard_map/ppermute | solution.py:18
  69.6 8.6 %collective-permute-start.16 = (bf16[2,2,256,128]{3,2,1,0:T(8,128)(2,1)S(1)}, bf16[2,2,256,128]{3,2,1,0:T(8,128)(2,1)S(1)}, u32[]{:S(2)}, u32[]{:S(2)}) collective-permute-start(bf16[2,2,256,128]{3,2,1,0:T(8,128)(2,1)S(1)} %collective-permute-done.15), channel_id=1, source_target_pairs={{0,32},{32,64},{64,96},{96,128},{128,160},{160,192},{192,224},{224... | collective-permute-start | bytes 786440 | tf_op jit(solution)/shard_map/ppermute | solution.py:18
  69.6 36.3 %collective-permute-start.21 = (bf16[2048,256]{1,0:T(8,128)(2,1)}, bf16[2048,256]{1,0:T(8,128)(2,1)S(1)}, u32[]{:S(2)}, u32[]{:S(2)}) collective-permute-start(bf16[2048,256]{1,0:T(8,128)(2,1)} %all-gather.4.cloned.1.call-done.weight), channel_id=1, source_target_pairs={{0,16},{16,0},{1,17},{17,1},{2,18},{18,2},{3,19},{19,3},{4,20},{20... | collective-permute-start | bytes 3145736 | tf_op jit(solution)/shard_map/ppermute | solution.py:18
  70.7 8.6 %collective-permute-start.13 = (bf16[2,2,256,128]{3,2,1,0:T(8,128)(2,1)S(1)}, bf16[2,2,256,128]{3,2,1,0:T(8,128)(2,1)S(1)}, u32[]{:S(2)}, u32[]{:S(2)}) collective-permute-start(bf16[2,2,256,128]{3,2,1,0:T(8,128)(2,1)S(1)} %collective-permute-done.12), channel_id=1, source_target_pairs={{0,224},{32,0},{64,32},{96,64},{128,96},{160,128},{192,160},{224,1... | collective-permute-start | bytes 786440 | tf_op jit(solution)/shard_map/ppermute | solution.py:18
  79.3 11.2 %collective-permute-start.14 = (bf16[2,2,256,128]{3,2,1,0:T(8,128)(2,1)S(1)}, bf16[2,2,256,128]{3,2,1,0:T(8,128)(2,1)S(1)}, u32[]{:S(2)}, u32[]{:S(2)}) collective-permute-start(bf16[2,2,256,128]{3,2,1,0:T(8,128)(2,1)S(1)} %collective-permute-done.13), channel_id=1, source_target_pairs={{0,224},{32,0},{64,32},{96,64},{128,96},{160,128},{192,160},{224,1... | collective-permute-start | bytes 786440 | tf_op jit(solution)/shard_map/ppermute | solution.py:18
  85.9 8.7 %collective-permute-start.18 = (bf16[1,2,256,128]{3,2,1,0:T(8,128)(2,1)S(1)}, bf16[1,2,256,128]{3,2,1,0:T(8,128)(2,1)S(1)}, u32[]{:S(2)}, u32[]{:S(2)}) collective-permute-start(bf16[1,2,256,128]{3,2,1,0:T(8,128)(2,1)S(1)} %get-tuple-element.31), channel_id=1, source_target_pairs={{0,32},{32,64},{64,96},{96,128},{128,160},{160,192},{192,224},{224... | collective-permute-start | bytes 393224 | tf_op jit(solution)/shard_map/ppermute | solution.py:18
  107.3 20.5 %collective-permute-start.22 = (bf16[8,256,256]{2,1,0:T(8,128)(2,1)S(1)}, bf16[8,256,256]{2,1,0:T(8,128)(2,1)S(1)}, u32[]{:S(2)}, u32[]{:S(2)}) collective-permute-start(bf16[8,256,256]{2,1,0:T(8,128)(2,1)S(1)} %get-tuple-element.22), channel_id=1, source_target_pairs={{0,1},{1,0},{2,3},{3,2},{4,5},{5,4},{6,7},{7,6},{8,9},{9,8},{10,11... | collective-permute-start | bytes 3145736 | tf_op jit(solution)/shard_map/ppermute | solution.py:18
  129.1 20.6 %all-to-all-start = ((bf16[8,256,256]{2,1,0:T(8,128)(2,1)}), bf16[8,256,256]{2,1,0:T(8,128)(2,1)S(1)}, u32[]{:S(2)}, u32[]{:S(2)}) async-start(bf16[8,256,256]{2,1,0:T(8,128)(2,1)} %add_convert_fusion.1), calls=%async_computation | async-start | bytes 2097152 | tf_op jit(solution)/shard_map/all_to_all | solution.py:202
  135.1 74.3 %all-gather.8.cloned.1.call-start = ((), (), s32[]{:S(2)}) async-start(), calls=%async_computation.5 | async-start | bytes 1179648 | tf_op jit(solution)/shard_map/all_gather | solution.py:234
  135.9 73.5 %collective-permute-start.24 = (bf16[2,2048,256]{2,1,0:T(8,128)(2,1)}, bf16[2,2048,256]{2,1,0:T(8,128)(2,1)}, u32[]{:S(2)}, u32[]{:S(2)}) collective-permute-start(bf16[2,2048,256]{2,1,0:T(8,128)(2,1)} %all-gather.6.cloned.1.call-done.weight), channel_id=1, source_target_pairs={{0,16},{16,0},{1,17},{17,1},{2,18},{18,2},{3,19},{19,3},{4,20},{20... | collective-permute-start | bytes 6291464 | tf_op jit(solution)/shard_map/ppermute | solution.py:18
  209.4 25.2 %collective-permute-start.27 = (bf16[2048,256]{1,0:T(8,128)(2,1)}, bf16[2048,256]{1,0:T(8,128)(2,1)S(1)}, u32[]{:S(2)}, u32[]{:S(2)}) collective-permute-start(bf16[2048,256]{1,0:T(8,128)(2,1)} %all-gather.8.cloned.1.call-done.weight), channel_id=1, source_target_pairs={{0,16},{16,0},{1,17},{17,1},{2,18},{18,2},{3,19},{19,3},{4,20},{20... | collective-permute-start | bytes 3145736 | tf_op jit(solution)/shard_map/ppermute | solution.py:18
  217.4 17.2 %collective-permute-start.25 = (bf16[16,256]{1,0:T(8,128)(2,1)S(1)}, bf16[16,256]{1,0:T(8,128)(2,1)S(1)}, u32[]{:S(2)}, u32[]{:S(2)}) collective-permute-start(bf16[16,256]{1,0:T(8,128)(2,1)S(1)} %get-tuple-element.42), channel_id=1, source_target_pairs={{0,16},{16,32},{32,48},{48,64},{64,80},{80,96},{96,112},{112,128},... | collective-permute-start | bytes 24584 | tf_op jit(solution)/shard_map/ppermute | solution.py:18
  217.5 17.3 %collective-permute-start.26 = (bf16[16,256]{1,0:T(8,128)(2,1)S(1)}, bf16[16,256]{1,0:T(8,128)(2,1)S(1)}, u32[]{:S(2)}, u32[]{:S(2)}) collective-permute-start(bf16[16,256]{1,0:T(8,128)(2,1)S(1)} %get-tuple-element.41), channel_id=1, source_target_pairs={{0,240},{16,0},{32,16},{48,32},{64,48},{80,64},{96,80},{112,96},{1... | collective-permute-start | bytes 24584 | tf_op jit(solution)/shard_map/ppermute | solution.py:18
  (21 other events, 352.9 us)
Sparse Core Ops, SparseCore 0:
  24.8 37.9 all-gather.3
  66.1 50.6 all-gather.5
  137.8 34.5 all-gather.7
